TPU v7x, 1024 devices: a whole 4x8x16 slice. The times are simulated.
1024 devices in a mesh: grp: 8 (over y), dev: 128 (over x, z, core).
Axes of the slice: x: 4, y: 8, z: 16, core: 2. Of those that a mesh axis runs over, the one named last changes fastest.
Arguments:
- gcm_state: float32 [2048, 3, 1152], P(('grp', 'dev')), may hold values from -6 to 6
- element_op: float32 [2048, 16, 16], P(('grp', 'dev')), may hold values from -1.5 to 1.5
- neighbours: int32 [2048, 4], P(('grp', 'dev')), may hold values from 0 to 2047, as said below
- crm_state: bfloat16 [40960, 2, 3712], P(('grp', 'dev')), may hold values from -6 to 6
- assignment: int32 [32768], P(('grp', 'dev')), may hold values from 0 to 5119, as said below
- column_cost: int32 [32768], P(('grp', 'dev')), may hold values from 1 to 4
Outputs:
- gcm_out: float32 [2048, 3, 1152], P(('grp', 'dev'))
- crm_out: bfloat16 [40960, 2, 3712], P(('grp', 'dev'))
Inputs may be any that keep to these rules, and one draw needn't show every extreme that they name: Entry [e, d] is the element across edge d of element e (0 east, 1 north, 2 west, 3 south); that element's edge (d + 2) % 4 meets it point for point in the same order. East and west neighbours lie in e's own block of 2 elements (rows e // 2), north ones in the next block and south ones in the previous block, cyclically over all blocks; the north neighbour of the east neighbour is the east neighbour of the north neighbour, and likewise at every corner. `assignment`: column c belongs to the group of 128 devices along dev that holds it; its value v names device v // 40 of that group and slot v % 40 there. No two columns of a group share a slot; columns go in pairs, so each device sends an even number of columns to each device; each device sends at most 2 columns to one device, some device sends exactly 2 to one, and some device's 40 slots are all filled.
All inputs are finite; a program needn't handle non-finite values.
Results may differ from a plain program's by a relative error of at most 0.0034.
Values may be sent and summed in bfloat16 or wider, within the bound.
A program may use at most 32 MiB of HBM per device.

v0:
```python
import jax
import jax.numpy as jnp
from jax import lax
from jax.sharding import PartitionSpec as P

NLEV = 72
CZ = 58
CX = 64
NSUB = 4
NDYN = 3


RELAX_RATE = 0.3
HORIZONTAL_MIX = 0.2
VERTICAL_MIX = 0.2
CONDENSE_RATE = 0.5
SATURATION_SLOPE = 0.2
UPPER_DAMPING = 0.5
DYNAMICS_STEP = 0.5


def with_halo(value, sides, width):
    for axis, dim in sides:
        devices, length = (lax.axis_size(axis), value.shape[dim])
        up = [(i, (i + 1) % devices) for i in range(devices)]
        down = [(j, i) for i, j in up]
        last = lax.slice_in_dim(value, length - width, length, axis=dim)
        leading = lax.slice_in_dim(value, 0, width, axis=dim)
        before = lax.ppermute(last, axis, up)
        after = lax.ppermute(leading, axis, down)
        value = jnp.concatenate([before, value, after], axis=dim)
    return value


def level_means(flat_fields):
    shape = flat_fields.shape
    return jnp.mean(flat_fields.reshape(shape[:-1] + (CZ, CX)), axis=-1)


def cloud_model(crm_in, forcing, step_counts, occupied):
    width = CZ * CX
    flat_ids = jnp.arange(width, dtype=jnp.int32)
    column_ids = flat_ids % CX
    level_ids = flat_ids // CX
    level_frac = level_ids.astype(jnp.float32) / CZ
    first_col = column_ids == 0
    last_col = column_ids == CX - 1
    top_level = level_ids == CZ - 1
    bottom_level = level_ids == 0
    fields = crm_in.astype(jnp.float32)
    start_mean = level_means(fields)
    forcing_drive = RELAX_RATE * (forcing[:, 0:2, :CZ] - start_mean)
    drive_flat = jnp.repeat(forcing_drive, CX, axis=-1)
    for substep in range(NSUB):
        left_side = jnp.where(
            first_col, jnp.roll(fields, -(CX - 1), axis=-1), jnp.roll(fields, 1, axis=-1)
        )
        right_side = jnp.where(
            last_col, jnp.roll(fields, CX - 1, axis=-1), jnp.roll(fields, -1, axis=-1)
        )
        across = left_side + right_side - 2.0 * fields
        upward = jnp.where(top_level, fields, jnp.roll(fields, -CX, axis=-1))
        downward = jnp.where(bottom_level, fields, jnp.roll(fields, CX, axis=-1))
        vertical = upward + downward - 2.0 * fields
        stepped = fields + drive_flat + HORIZONTAL_MIX * across + VERTICAL_MIX * vertical
        saturated = 0.5 - 0.8 * level_frac[None, :] + SATURATION_SLOPE * stepped[:, 0]
        excess = jax.nn.relu(stepped[:, 1] - saturated)
        stepped = stepped + jnp.stack([CONDENSE_RATE * excess, -CONDENSE_RATE * excess], axis=1)
        active = (substep < step_counts)[:, None, None]
        fields = jnp.where(active, stepped, fields)
    end_mean = level_means(fields)
    final_sat = 0.5 - 0.8 * level_frac[None, :] + SATURATION_SLOPE * fields[:, 0]
    cloud_water = level_means(jax.nn.relu(fields[:, 1] - final_sat))
    lower_tend = jnp.concatenate(
        [end_mean - start_mean, (cloud_water - forcing[:, 2, :CZ])[:, None]], axis=1
    )
    occupied_mask = (occupied > 0.5)[:, None, None]
    new_state = jnp.where(occupied_mask, fields.astype(jnp.bfloat16), crm_in)
    return (lower_tend, new_state)


def assemble(
    point_grid, north_row, south_row, east_col, west_col, corner_ne, corner_nw, corner_se, corner_sw
):
    combined = point_grid.at[:, :, 3].add(north_row)
    combined = combined.at[:, :, 0].add(south_row)
    combined = combined.at[:, :, :, 3].add(east_col)
    combined = combined.at[:, :, :, 0].add(west_col)
    combined = combined.at[:, :, 3, 3].add(corner_ne)
    combined = combined.at[:, :, 3, 0].add(corner_nw)
    combined = combined.at[:, :, 0, 3].add(corner_se)
    combined = combined.at[:, :, 0, 0].add(corner_sw)
    multiplicity = jnp.array([2.0, 1.0, 1.0, 2.0], dtype=jnp.float32)
    weight = 1.0 / (multiplicity[:, None] * multiplicity[None, :])
    return combined * weight[None, None, :, :, None]


def body(gcm_state, element_op, neighbours, crm_state, assignment, column_cost):
    elements = gcm_state.shape[0]
    columns_here = assignment.shape[0]
    slots_here = crm_state.shape[0]
    peer_count = lax.axis_size("dev")
    capacity = 2 * ((columns_here + peer_count - 1) // peer_count)
    sent_levels = NLEV
    state_round = gcm_state.astype(jnp.bfloat16)
    columns = (
        state_round.reshape(elements, 3, 16, NLEV)
        .transpose(0, 2, 1, 3)
        .reshape(columns_here, 3, NLEV)
    )
    payload = columns.reshape(columns_here, 3 * sent_levels)
    target = assignment // slots_here
    slot_here = assignment % slots_here
    order_ids = jnp.arange(columns_here, dtype=jnp.int32)
    earlier = (target[:, None] == target[None, :]) & (order_ids[None, :] < order_ids[:, None])
    rank_ids = jnp.sum(earlier.astype(jnp.int32), axis=1)
    buffer_ids = target * capacity + rank_ids
    row_ids = jnp.arange(peer_count * capacity, dtype=jnp.int32)
    packer = row_ids[:, None] == buffer_ids[None, :]
    packer_half = packer.astype(jnp.bfloat16)
    packed = jnp.dot(packer_half, payload, preferred_element_type=jnp.float32).astype(jnp.bfloat16)
    labels = jnp.stack([slot_here + 1, column_cost], axis=1)
    packed_labels = jnp.dot(packer.astype(jnp.int32), labels)
    arrived, arrived_labels = (
        lax.all_to_all(
            packed.reshape(peer_count, capacity, 3 * sent_levels),
            "dev",
            split_axis=0,
            concat_axis=0,
            tiled=True,
        ),
        lax.all_to_all(
            packed_labels.reshape(peer_count, capacity, 2),
            "dev",
            split_axis=0,
            concat_axis=0,
            tiled=True,
        ),
    )
    local_ids = neighbours % elements
    east_ids = local_ids[:, 0]
    north_ids = local_ids[:, 1]
    west_ids = local_ids[:, 2]
    south_ids = local_ids[:, 3]
    dynamic = gcm_state
    for update_index in range(NDYN):
        tendency = jnp.einsum(
            "epq,efqk->efpk",
            element_op,
            dynamic.reshape(elements, 3, 16, NLEV),
            precision=lax.Precision.HIGHEST,
        )
        point_grid = tendency.reshape(elements, 3, 4, 4, NLEV)
        edge_rows = jnp.stack([point_grid[:, :, 0], point_grid[:, :, 3]], axis=0)
        extended = with_halo(edge_rows, ((("grp", "dev"), 0),), 1)
        below_north = extended[0]
        above_south = extended[3]
        summed = assemble(
            point_grid,
            above_south[north_ids],
            below_north[south_ids],
            point_grid[east_ids][:, :, :, 0],
            point_grid[west_ids][:, :, :, 3],
            above_south[north_ids[east_ids]][:, :, 0],
            above_south[north_ids[west_ids]][:, :, 3],
            below_north[south_ids[east_ids]][:, :, 0],
            below_north[south_ids[west_ids]][:, :, 3],
        )
        dynamic = dynamic + DYNAMICS_STEP * summed.reshape(dynamic.shape)
    flat_rows = arrived.reshape(peer_count * capacity, 3 * sent_levels)
    flat_labels = arrived_labels.reshape(peer_count * capacity, 2)
    slot_range = jnp.arange(slots_here, dtype=jnp.int32)
    matcher = slot_range[:, None] == (flat_labels[:, 0] - 1)[None, :]
    matcher_half = matcher.astype(jnp.bfloat16)
    forcing = jnp.dot(matcher_half, flat_rows, preferred_element_type=jnp.float32).reshape(
        slots_here, 3, sent_levels
    )
    occupied = jnp.sum(matcher.astype(jnp.float32), axis=1)
    step_counts = jnp.dot(matcher.astype(jnp.int32), flat_labels[:, 1])
    lower_tend, crm_out = cloud_model(crm_state, forcing, step_counts, occupied)
    slot_tend = jnp.concatenate([lower_tend, -UPPER_DAMPING * forcing[:, :, CZ:]], axis=2).astype(
        jnp.bfloat16
    )
    back_rows = jnp.dot(
        matcher_half.T,
        slot_tend.reshape(slots_here, 3 * sent_levels),
        preferred_element_type=jnp.float32,
    ).astype(jnp.bfloat16)
    returned = lax.all_to_all(
        back_rows.reshape(peer_count, capacity, 3 * sent_levels),
        "dev",
        split_axis=0,
        concat_axis=0,
        tiled=True,
    )
    col_tend = jnp.dot(
        packer_half.T,
        returned.reshape(peer_count * capacity, 3 * sent_levels),
        preferred_element_type=jnp.float32,
    ).reshape(columns_here, 3, sent_levels)
    tend_grid = (
        col_tend.reshape(elements, 16, 3, NLEV).transpose(0, 2, 1, 3).reshape(gcm_state.shape)
    )
    return (dynamic + tend_grid, crm_out)


def solution(mesh):
    in_specs = (
        P(("grp", "dev"), None, None),
        P(("grp", "dev"), None, None),
        P(("grp", "dev"), None),
        P(("grp", "dev"), None, None),
        P(("grp", "dev")),
        P(("grp", "dev")),
    )
    out_specs = (P(("grp", "dev"), None, None), P(("grp", "dev"), None, None))
    return jax.shard_map(body, mesh=mesh, in_specs=in_specs, out_specs=out_specs, check_vma=False)
```

profile of v0, /device:TPU:1, one launch (start us, length us, event | category | flops | bytes accessed | tf_op | source)
XLA Modules:
  0.0 181.2 jit_solution(15699328187082442261)
XLA Ops:
  0.6 0.9 reshape.1306
  1.7 16.1 %collective-permute-start = (f32[1,2,3,4,72]{4,3,2,1,0:T(4,128)S(1)}, f32[1,2,3,4,72]{4,3,2,1,0:T(4,128)S(1)}, u32[]{:S(2)}, u32[]{:S(2)}) collective-permute-start(f32[1,2,3,4,72]{4,3,2,1,0:T(4,128)S(1)} %slice_bitcast_fusion.2), channel_id=1, source_target_pairs={{1,0},{2,1},{3,2},{4,3},{5,4},{6,5},{7,6},{8,7},{9,8},{10,9},{11,1... | collective-permute-start | bytes 20744 | tf_op jit(solution)/shard_map/ppermute | solution.py:30
  17.8 0.7 fusion.106
  18.6 0.8 fusion.47
  19.6 0.8 copy.96
  20.4 13.5 %all-to-all-start = ((s32[128,2,2]{1,2,0:T(2,128)}), s32[128,2,2]{1,2,0:T(2,128)S(1)}, u32[]{:S(2)}, u32[]{:S(2)}) async-start(s32[128,2,2]{1,2,0:T(2,128)} %copy.96), calls=%async_computation | async-start | bytes 262144 | tf_op jit(solution)/shard_map/all_to_all | solution.py:132
  33.9 0.8 copy.88
  37.4 1.5 fusion.135
  38.9 1.8 fusion.136
  40.7 1.8 %fusion.139 = (f32[40,2,3649]{2,0,1:T(8,128)}, f32[40,2,3649]{2,0,1:T(8,128)}) fusion(f32[40,2,3712]{2,0,1:T(8,128)S(1)} %copy_convert_fusion), kind=kLoop, calls=%fused_computation.302 | loop fusion | bytes 4670720 | tf_op jit(solution)/shard_map/jit(_roll_static)/slice | solution.py:59
  42.6 0.7 fusion.138
  44.0 0.7 iota_compare_fusion.6
  47.2 0.8 and_reduce_fusion
  48.6 1.2 gather_fusion.2
  50.3 2.5 %reshape.1337 = f32[40,2,58,64]{3,2,0,1:T(8,128)} reshape(f32[40,2,3712]{2,0,1:T(8,128)S(1)} %copy_convert_fusion) | data formatting | bytes 2375680 | tf_op jit(solution)/shard_map/reshape | solution.py:37
  52.9 2.5 %reduce_sum.46 = f32[40,2,58]{2,0,1:T(8,128)S(1)} reduce(f32[40,2,58,64]{3,2,0,1:T(8,128)} %reshape.1337, f32[]{:T(128)} %constant.655.clone.1), dimensions={3}, to_apply=%region_2.3 | reduce | flops 292320 | bytes 1206404 | tf_op jit(solution)/shard_map/reduce_sum | solution.py:37
  56.0 3.5 %collective-permute-start.1 = (f32[1,2,3,4,72]{4,3,2,1,0:T(4,128)S(1)}, f32[1,2,3,4,72]{4,3,2,1,0:T(4,128)S(1)}, u32[]{:S(2)}, u32[]{:S(2)}) collective-permute-start(f32[1,2,3,4,72]{4,3,2,1,0:T(4,128)S(1)} %get-tuple-element.362), channel_id=1, source_target_pairs={{0,1},{1,2},{2,3},{3,4},{4,5},{5,6},{6,7},{7,8},{8,9},{9,10},{10,1... | collective-permute-start | bytes 20744 | tf_op jit(solution)/shard_map/ppermute | solution.py:29
  60.1 0.7 gather_fusion.7
  61.0 0.7 gather_fusion.1
  61.7 0.8 slice_add_fusion.7
  62.9 0.7 gather_fusion.9
  63.6 2.0 %broadcast_select_fusion.2 = f32[2,3,1,1,72]{4,3,2,1,0:T(1,128)S(1)} fusion(pred[]{:T(512)} %and_reduce_fusion, f32[2,3,4,72]{3,2,1,0:T(4,128)S(1)} %gather_fusion.9, f32[2,3,4,4,72]{4,3,2,1,0:T(4,128)S(1)} %scatter-add.89, s32[]{:T(128)} %bitcast.22, s32[]{:T(128)} %bitcast.23), kind=kLoop, calls=%fused_computation.209 | loop fusion | flops 864 | bytes 5193 | tf_op jit(solution)/shard_map/select.30
  65.5 1.3 scatter-add.90
  66.8 0.7 gather_fusion.11
  68.1 8.3 %collective-permute-start.2 = (f32[1,2,3,4,72]{4,3,2,1,0:T(4,128)S(1)}, f32[1,2,3,4,72]{4,3,2,1,0:T(4,128)S(1)}, u32[]{:S(2)}, u32[]{:S(2)}) collective-permute-start(f32[1,2,3,4,72]{4,3,2,1,0:T(4,128)S(1)} %slice_bitcast_fusion.1), channel_id=1, source_target_pairs={{1,0},{2,1},{3,2},{4,3},{5,4},{6,5},{7,6},{8,7},{9,8},{10,9},{11,1... | collective-permute-start | bytes 20744 | tf_op jit(solution)/shard_map/ppermute | solution.py:30
  77.8 0.7 gather_fusion.12
  78.5 1.9 %collective-permute-start.3 = (f32[1,2,3,4,72]{4,3,2,1,0:T(4,128)S(1)}, f32[1,2,3,4,72]{4,3,2,1,0:T(4,128)S(1)}, u32[]{:S(2)}, u32[]{:S(2)}) collective-permute-start(f32[1,2,3,4,72]{4,3,2,1,0:T(4,128)S(1)} %get-tuple-element.360), channel_id=1, source_target_pairs={{0,1},{1,2},{2,3},{3,4},{4,5},{5,6},{6,7},{7,8},{8,9},{9,10},{10,1... | collective-permute-start | bytes 20744 | tf_op jit(solution)/shard_map/ppermute | solution.py:29
  80.6 0.7 gather_fusion.16
  81.3 0.7 gather_fusion.17
  82.0 0.7 gather_fusion.13
  82.7 0.7 gather_fusion.18
  83.4 0.7 gather_fusion.19
  84.4 2.0 %broadcast_select_fusion.1 = f32[2,3,1,1,72]{4,3,2,1,0:T(1,128)S(1)} fusion(pred[]{:T(512)} %and_reduce_fusion, f32[2,3,4,72]{3,2,1,0:T(4,128)S(1)} %gather_fusion.18, f32[2,3,4,4,72]{4,3,2,1,0:T(4,128)S(1)} %scatter-add.101, s32[]{:T(128)} %bitcast.22, s32[]{:T(128)} %bitcast.23), kind=kLoop, calls=%fused_computation.208 | loop fusion | flops 864 | bytes 5193 | tf_op jit(solution)/shard_map/select.38
  86.4 1.3 scatter-add.104
  88.3 9.1 %collective-permute-start.4 = (f32[1,2,3,4,72]{4,3,2,1,0:T(4,128)S(1)}, f32[1,2,3,4,72]{4,3,2,1,0:T(4,128)S(1)}, u32[]{:S(2)}, u32[]{:S(2)}) collective-permute-start(f32[1,2,3,4,72]{4,3,2,1,0:T(4,128)S(1)} %slice_bitcast_fusion), channel_id=1, source_target_pairs={{1,0},{2,1},{3,2},{4,3},{5,4},{6,5},{7,6},{8,7},{9,8},{10,9},{11,1... | collective-permute-start | bytes 20744 | tf_op jit(solution)/shard_map/ppermute | solution.py:30
  97.6 0.7 gather_fusion.22
  98.3 0.7 gather_fusion.23
  99.0 0.7 gather_fusion.20
  99.7 1.9 %collective-permute-start.5 = (f32[1,2,3,4,72]{4,3,2,1,0:T(4,128)S(1)}, f32[1,2,3,4,72]{4,3,2,1,0:T(4,128)S(1)}, u32[]{:S(2)}, u32[]{:S(2)}) collective-permute-start(f32[1,2,3,4,72]{4,3,2,1,0:T(4,128)S(1)} %get-tuple-element.358), channel_id=1, source_target_pairs={{0,1},{1,2},{2,3},{3,4},{4,5},{5,6},{6,7},{7,8},{8,9},{9,10},{10,1... | collective-permute-start | bytes 20744 | tf_op jit(solution)/shard_map/ppermute | solution.py:29
  102.0 0.7 reshape.1335
  102.8 7.4 %all-to-all-start.1 = ((bf16[128,2,216]{2,1,0:T(2,128)(2,1)}), bf16[128,2,216]{2,1,0:T(2,128)(2,1)S(1)}, u32[]{:S(2)}, u32[]{:S(2)}) async-start(bf16[128,2,216]{2,1,0:T(2,128)(2,1)} %reshape.1335), calls=%async_computation.1 | async-start | bytes 262144 | tf_op jit(solution)/shard_map/all_to_all | solution.py:125
  110.1 0.7 gather_fusion.24
  110.8 0.7 gather_fusion.25
  111.5 0.7 gather_fusion.21
  112.2 0.7 gather_fusion.26
  112.9 1.3 gather_fusion.27
  114.6 2.0 %broadcast_select_fusion = f32[2,3,1,1,72]{4,3,2,1,0:T(1,128)S(1)} fusion(pred[]{:T(512)} %and_reduce_fusion, f32[2,3,4,72]{3,2,1,0:T(4,128)S(1)} %gather_fusion.26, f32[2,3,4,4,72]{4,3,2,1,0:T(4,128)S(1)} %scatter-add.115, s32[]{:T(128)} %bitcast.22, s32[]{:T(128)} %bitcast.23), kind=kLoop, calls=%fused_computation.207 | loop fusion | flops 864 | bytes 5193 | tf_op jit(solution)/shard_map/select.46
  116.5 1.3 scatter-add.116
  117.8 9.7 %all-to-all-done.1 = bf16[128,2,216]{2,1,0:T(2,128)(2,1)S(1)} async-done(((bf16[128,2,216]{2,1,0:T(2,128)(2,1)}), bf16[128,2,216]{2,1,0:T(2,128)(2,1)S(1)}, u32[]{:S(2)}, u32[]{:S(2)}) %all-to-all-start.1) | async-done | bytes 110624 | tf_op jit(solution)/shard_map/all_to_all | solution.py:125
  128.0 1.9 %broadcast_in_dim.151 = f32[40,2,58,64]{3,2,0,1:T(8,128)} broadcast(f32[40,2,58]{2,0,1:T(8,128)S(1)} %fusion.57), dimensions={0,1,2} | broadcast | bytes 1206400 | tf_op jit(solution)/shard_map/broadcast_in_dim | solution.py:53
  129.9 2.4 %reshape.1338 = f32[40,2,3712]{2,0,1:T(8,128)S(1)} reshape(f32[40,2,58,64]{3,2,0,1:T(8,128)} %broadcast_in_dim.151) | data formatting | bytes 2375680 | tf_op jit(solution)/shard_map/reshape | solution.py:53
  132.4 3.8 %fusion.4 = f32[40,2,3712]{2,0,1:T(8,128)S(1)} fusion(f32[40,2,3712]{2,0,1:T(8,128)S(1)} %reshape.1338, f32[40,2,63]{2,0,1:T(8,128)S(1)} %copy-done.4, f32[40,2,3649]{2,0,1:T(8,128)} %get-tuple-element.357, f32[40,2,3711]{2,0,1:T(8,128)} %get-tuple-element.351, f32[40,2,1]{2,0,1:T(8,128)S(1)} %get-tuple-element.353, f32[40,2,3649]{2,0,1:T(8,128)} %get-tuple-element.356, ...), kind=kLoop, calls=%fused_computation.38 | loop fusion | flops 6236160 | bytes 10111488 | tf_op jit(solution)/shard_map/add | solution.py:65
  138.0 1.3 fusion.12
  141.1 1.4 fusion.21
  144.3 1.3 fusion.30
  145.8 1.2 convert_select_fusion.3
  146.9 2.5 %reshape.1339 = f32[40,2,58,64]{3,2,0,1:T(8,128)} reshape(f32[40,2,3712]{2,0,1:T(8,128)S(1)} %get-tuple-element.299) | data formatting | bytes 2375680 | tf_op jit(solution)/shard_map/reshape | solution.py:37
  149.6 2.5 %reduce_sum.47 = f32[40,2,58]{2,0,1:T(8,128)S(1)} reduce(f32[40,2,58,64]{3,2,0,1:T(8,128)} %reshape.1339, f32[]{:T(128)} %constant.655.clone.1), dimensions={3}, to_apply=%region_3.4 | reduce | flops 292320 | bytes 1206404 | tf_op jit(solution)/shard_map/reduce_sum | solution.py:37
  152.1 0.8 mul.293
  154.8 0.7 reshape.1340
  155.5 6.9 %all-to-all-start.2 = ((bf16[128,2,216]{2,1,0:T(2,128)(2,1)}), bf16[128,2,216]{2,1,0:T(2,128)(2,1)S(1)}, u32[]{:S(2)}, u32[]{:S(2)}) async-start(bf16[128,2,216]{2,1,0:T(2,128)(2,1)} %reshape.1340), calls=%async_computation.2 | async-start | bytes 262144 | tf_op jit(solution)/shard_map/all_to_all | solution.py:189
  162.4 0.7 fusion.91
  163.4 1.3 copy.107
  164.6 15.4 %all-to-all-done.2 = bf16[128,2,216]{2,1,0:T(2,128)(2,1)S(1)} async-done(((bf16[128,2,216]{2,1,0:T(2,128)(2,1)}), bf16[128,2,216]{2,1,0:T(2,128)(2,1)S(1)}, u32[]{:S(2)}, u32[]{:S(2)}) %all-to-all-start.2) | async-done | bytes 110624 | tf_op jit(solution)/shard_map/all_to_all | solution.py:189
  (183 shorter events, 22.3 us)
Async XLA Ops:
  0.6 0.9 copy-start
  1.7 53.7 %collective-permute-start = (f32[1,2,3,4,72]{4,3,2,1,0:T(4,128)S(1)}, f32[1,2,3,4,72]{4,3,2,1,0:T(4,128)S(1)}, u32[]{:S(2)}, u32[]{:S(2)}) collective-permute-start(f32[1,2,3,4,72]{4,3,2,1,0:T(4,128)S(1)} %slice_bitcast_fusion.2), channel_id=1, source_target_pairs={{1,0},{2,1},{3,2},{4,3},{5,4},{6,5},{7,6},{8,7},{9,8},{10,9},{11,1... | collective-permute-start | bytes 20744 | tf_op jit(solution)/shard_map/ppermute | solution.py:30
  18.6 25.4 %copy-start.14 = (s32[32]{0:T(128)}, s32[32]{0:T(128)S(1)}, u32[]{:S(2)}) copy-start(s32[32]{0:T(128)S(1)} %multiply_add_fusion.1) | copy-start | bytes 388
  20.4 16.9 %copy-start.1 = (bf16[40,2,3712]{2,1,0:T(2,128)(2,1)S(1)}, bf16[40,2,3712]{2,1,0:T(2,128)(2,1)}, u32[]{:S(2)}) copy-start(bf16[40,2,3712]{2,1,0:T(2,128)(2,1)} %param.60) | copy-start | bytes 1781764
  20.4 40.4 %all-to-all-start = ((s32[128,2,2]{1,2,0:T(2,128)}), s32[128,2,2]{1,2,0:T(2,128)S(1)}, u32[]{:S(2)}, u32[]{:S(2)}) async-start(s32[128,2,2]{1,2,0:T(2,128)} %copy.96), calls=%async_computation | async-start | bytes 262144 | tf_op jit(solution)/shard_map/all_to_all | solution.py:132
  34.7 41.9 %copy-start.8 = (s32[1024]{0:T(1024)}, s32[1024]{0:T(1024)S(1)}, u32[]{:S(2)}) copy-start(s32[1024]{0:T(1024)S(1)} %pad_clamp_fusion.5) | copy-start | bytes 12292
  34.7 42.5 %copy-start.9 = (s32[1024]{0:T(1024)}, s32[1024]{0:T(1024)S(1)}, u32[]{:S(2)}) copy-start(s32[1024]{0:T(1024)S(1)} %pad_clamp_fusion.4) | copy-start | bytes 12292
  40.7 6.5 %copy-start.16 = (f32[4]{0:T(128)S(1)}, f32[4]{0:T(128)}, u32[]{:S(2)}) copy-start(f32[4]{0:T(128)} %constant.666.clone) | copy-start | bytes 52
  40.7 6.5 %copy-start.17 = (s32[5]{0:T(128)S(1)}, s32[5]{0:T(128)}, u32[]{:S(2)}) copy-start(s32[5]{0:T(128)} %constant.649.clone.1) | copy-start | bytes 64
  44.7 10.7 %copy-start.13 = (s32[1024]{0:T(1024)}, s32[1024]{0:T(1024)S(1)}, u32[]{:S(2)}) copy-start(s32[1024]{0:T(1024)S(1)} %pad_clamp_fusion.7) | copy-start | bytes 12292
  45.3 14.3 %copy-start.12 = (s32[1024]{0:T(1024)}, s32[1024]{0:T(1024)S(1)}, u32[]{:S(2)}) copy-start(s32[1024]{0:T(1024)S(1)} %pad_clamp_fusion.3) | copy-start | bytes 12292
  52.9 14.9 %copy-start.6 = (f32[2,3,1152]{2,0,1:T(2,128)S(1)}, f32[2,3,1152]{2,0,1:T(2,128)}, u32[]{:S(2)}) copy-start(f32[2,3,1152]{2,0,1:T(2,128)} %param.57) | copy-start | bytes 82948
  56.0 5.0 %collective-permute-start.1 = (f32[1,2,3,4,72]{4,3,2,1,0:T(4,128)S(1)}, f32[1,2,3,4,72]{4,3,2,1,0:T(4,128)S(1)}, u32[]{:S(2)}, u32[]{:S(2)}) collective-permute-start(f32[1,2,3,4,72]{4,3,2,1,0:T(4,128)S(1)} %get-tuple-element.362), channel_id=1, source_target_pairs={{0,1},{1,2},{2,3},{3,4},{4,5},{5,6},{6,7},{7,8},{8,9},{9,10},{10,1... | collective-permute-start | bytes 20744 | tf_op jit(solution)/shard_map/ppermute | solution.py:29
  61.0 66.8 %copy-start.10 = (s32[256,1]{0,1:T(1,128)}, s32[256,1]{0,1:T(1,128)S(1)}, u32[]{:S(2)}) copy-start(s32[256,1]{0,1:T(1,128)S(1)} %slice_add_fusion.9) | copy-start | bytes 3076
  61.7 39.9 %copy-start.15 = (s32[32]{0:T(128)S(1)}, s32[32]{0:T(128)}, u32[]{:S(2)}) copy-start(s32[32]{0:T(128)} %copy-done.14) | copy-start | bytes 388
  68.1 9.7 %collective-permute-start.2 = (f32[1,2,3,4,72]{4,3,2,1,0:T(4,128)S(1)}, f32[1,2,3,4,72]{4,3,2,1,0:T(4,128)S(1)}, u32[]{:S(2)}, u32[]{:S(2)}) collective-permute-start(f32[1,2,3,4,72]{4,3,2,1,0:T(4,128)S(1)} %slice_bitcast_fusion.1), channel_id=1, source_target_pairs={{1,0},{2,1},{3,2},{4,3},{5,4},{6,5},{7,6},{8,7},{9,8},{10,9},{11,1... | collective-permute-start | bytes 20744 | tf_op jit(solution)/shard_map/ppermute | solution.py:30
  78.5 3.4 %collective-permute-start.3 = (f32[1,2,3,4,72]{4,3,2,1,0:T(4,128)S(1)}, f32[1,2,3,4,72]{4,3,2,1,0:T(4,128)S(1)}, u32[]{:S(2)}, u32[]{:S(2)}) collective-permute-start(f32[1,2,3,4,72]{4,3,2,1,0:T(4,128)S(1)} %get-tuple-element.360), channel_id=1, source_target_pairs={{0,1},{1,2},{2,3},{3,4},{4,5},{5,6},{6,7},{7,8},{8,9},{9,10},{10,1... | collective-permute-start | bytes 20744 | tf_op jit(solution)/shard_map/ppermute | solution.py:29
  88.3 10.7 %collective-permute-start.4 = (f32[1,2,3,4,72]{4,3,2,1,0:T(4,128)S(1)}, f32[1,2,3,4,72]{4,3,2,1,0:T(4,128)S(1)}, u32[]{:S(2)}, u32[]{:S(2)}) collective-permute-start(f32[1,2,3,4,72]{4,3,2,1,0:T(4,128)S(1)} %slice_bitcast_fusion), channel_id=1, source_target_pairs={{1,0},{2,1},{3,2},{4,3},{5,4},{6,5},{7,6},{8,7},{9,8},{10,9},{11,1... | collective-permute-start | bytes 20744 | tf_op jit(solution)/shard_map/ppermute | solution.py:30
  99.7 11.8 %collective-permute-start.5 = (f32[1,2,3,4,72]{4,3,2,1,0:T(4,128)S(1)}, f32[1,2,3,4,72]{4,3,2,1,0:T(4,128)S(1)}, u32[]{:S(2)}, u32[]{:S(2)}) collective-permute-start(f32[1,2,3,4,72]{4,3,2,1,0:T(4,128)S(1)} %get-tuple-element.358), channel_id=1, source_target_pairs={{0,1},{1,2},{2,3},{3,4},{4,5},{5,6},{6,7},{7,8},{8,9},{9,10},{10,1... | collective-permute-start | bytes 20744 | tf_op jit(solution)/shard_map/ppermute | solution.py:29
  102.8 24.8 %all-to-all-start.1 = ((bf16[128,2,216]{2,1,0:T(2,128)(2,1)}), bf16[128,2,216]{2,1,0:T(2,128)(2,1)S(1)}, u32[]{:S(2)}, u32[]{:S(2)}) async-start(bf16[128,2,216]{2,1,0:T(2,128)(2,1)} %reshape.1335), calls=%async_computation.1 | async-start | bytes 262144 | tf_op jit(solution)/shard_map/all_to_all | solution.py:125
  129.9 2.5 %copy-start.3 = (f32[40,2,63]{2,0,1:T(8,128)S(1)}, f32[40,2,63]{2,0,1:T(8,128)}, u32[]{:S(2)}) copy-start(f32[40,2,63]{2,0,1:T(8,128)} %get-tuple-element.354) | copy-start | bytes 60484
  129.9 2.5 %copy-start.4 = (f32[40,2,63]{2,0,1:T(8,128)S(1)}, f32[40,2,63]{2,0,1:T(8,128)}, u32[]{:S(2)}) copy-start(f32[40,2,63]{2,0,1:T(8,128)} %get-tuple-element.355) | copy-start | bytes 60484
  152.9 0.8 copy-start.5
  153.7 0.7 copy-start.11
  154.2 9.2 %copy-start.2 = (bf16[40,2,3712]{2,0,1:T(8,128)(2,1)S(1)}, bf16[40,2,3712]{2,0,1:T(8,128)(2,1)}, u32[]{:S(2)}) copy-start(bf16[40,2,3712]{2,0,1:T(8,128)(2,1)} %get-tuple-element.298) | copy-start | bytes 1781764
  154.8 25.5 %copy-start.7 = (pred[32,256]{1,0:T(8,128)(4,1)S(1)}, pred[32,256]{1,0:T(8,128)(4,1)}, u32[]{:S(2)}) copy-start(pred[32,256]{1,0:T(8,128)(4,1)} %iota_compare_fusion.6) | copy-start | bytes 24580
  155.5 24.5 %all-to-all-start.2 = ((bf16[128,2,216]{2,1,0:T(2,128)(2,1)}), bf16[128,2,216]{2,1,0:T(2,128)(2,1)S(1)}, u32[]{:S(2)}, u32[]{:S(2)}) async-start(bf16[128,2,216]{2,1,0:T(2,128)(2,1)} %reshape.1340), calls=%async_computation.2 | async-start | bytes 262144 | tf_op jit(solution)/shard_map/all_to_all | solution.py:189
where the time goes:
time: 182 us; the launch traced here: 181 us
  starting transfers between devices  68.6 us (38%)
  local copies, waits for them, and re-layouts  53.2 us (29%)
  other arithmetic  30.5 us (17%)
  waiting for transfers between devices  25.1 us (14%)
  matrix products  2.26 us (1%)
    ppermute x3, starting transfers between devices, with_halo(): after = lax.ppermute(leading, axis, down)  33.5 us
    all_to_all x1, waiting for transfers between devices, body(): lax.all_to_all(back_rows.reshape(peer_count, capacity, 3 * sent_levels),...  15.4 us
    all_to_all x1, starting transfers between devices, body(): lax.all_to_all(packed_labels.reshape(peer_count, capacity, 2), 'dev', spl...  13.5 us
    all_to_all x1, waiting for transfers between devices, body(): lax.all_to_all(packed.reshape(peer_count, capacity, 3 * sent_levels), 'de...  9.7 us
    add x4, other arithmetic, cloud_model(): fields + drive_flat + HORIZONTAL_MIX * across + VERTICAL_MIX * vertical  7.84 us
    ppermute x3, starting transfers between devices, with_halo(): before = lax.ppermute(last, axis, up)  7.38 us
    all_to_all x1, starting transfers between devices, body(): lax.all_to_all(packed.reshape(peer_count, capacity, 3 * sent_levels), 'de...  7.36 us
    all_to_all x1, starting transfers between devices, body(): lax.all_to_all(back_rows.reshape(peer_count, capacity, 3 * sent_levels),...  6.9 us
  transfers between devices with their start and end apart: 9, of which 2 were waited for; matrix products, arithmetic and copies ran while one was open for 23% of the time, Pallas kernels for 0%

commit v1 on v0

v1 whole, which is shorter than its diff:
```python
import functools

import jax
import jax.numpy as jnp
from jax import lax
from jax.experimental import pallas as pl
from jax.experimental.pallas import tpu as pltpu
from jax.sharding import PartitionSpec as P

NLEV = 72
CZ = 58
CX = 64
HALF = CZ // 2
NSUB = 4
NDYN = 3
COLS = 32
SLOTS = 40
LANES = 128
WIDE = HALF * LANES

MESH = pl.DeviceIdType.MESH
BF16 = jnp.bfloat16
F32 = jnp.float32

LANE_TARGET = 58
LANE_SLOT = 59
LANE_COST = 60


def iota(shape, axis):
    return lax.broadcasted_iota(jnp.int32, shape, axis)


def one_hot(mask, scale=1.0):
    return jnp.where(mask, scale, 0.0).astype(BF16)


def dot(a, b):
    return jnp.dot(a, b, preferred_element_type=F32)


def dot_nt(a, b):
    return lax.dot_general(a, b, (((1,), (1,)), ((), ())), preferred_element_type=F32)


def dot_full(a, b):
    return jnp.dot(a, b, precision=lax.Precision.HIGHEST, preferred_element_type=F32)


def edge_weights(nb_ref):
    shape = (COLS, 48)
    row, col = iota(shape, 0), iota(shape, 1)
    e, p = row // 16, row % 16
    j, i = p // 4, p % 4

    def pick(direction, which):
        first, second = nb_ref[0, direction] % 2, nb_ref[1, direction] % 2
        return jnp.where(which == 0, first, second)

    east, north, west, south = (pick(d, e) for d in range(4))
    side = jnp.where(i == 3, east, west)
    across = 3 - i
    inner = (i == 1) | (i == 2)
    upper, lower = j == 3, j == 0
    count = jnp.where(col == row, 1.0, 0.0)
    add = lambda total, mask: total + jnp.where(mask, 1.0, 0.0)
    count = add(count, ~inner & (col == side * 16 + j * 4 + across))
    count = add(count, upper & (col == 32 + north * 4 + i))
    count = add(count, lower & (col == 40 + south * 4 + i))
    count = add(count, upper & ~inner & (col == 32 + pick(1, side) * 4 + across))
    count = add(count, lower & ~inner & (col == 40 + pick(3, side) * 4 + across))
    share = jnp.where(inner, 1.0, 0.5) * jnp.where(upper | lower, 0.5, 1.0)
    return count * share * 0.5


def kernel(
    dims,
    gcm_ref,
    op_ref,
    nb_ref,
    crm_ref,
    asg_ref,
    cost_ref,
    gout_ref,
    cout_ref,
    dyn,
    base,
    near,
    edge_out,
    edge_in,
    got1,
    pack2,
    got2,
    pack3,
    got3,
    pack4,
    got4,
    state_a,
    state_b,
    drive,
    half_in,
    spread,
    tend,
    s1,
    r1,
    s2,
    r2,
    s3,
    r3,
    s4,
    r4,
    se,
    re,
):
    n_grp, nx, nz, cap = dims
    n_near = nx * 2
    n_dev = n_near * nz
    rows1 = n_near * COLS
    cap2 = cap * n_near
    rows2 = nz * cap2
    grp, dev = lax.axis_index("grp"), lax.axis_index("dev")
    core = dev % 2
    z = (dev // 2) % nz
    x = dev // (2 * nz)
    me = x * 2 + core
    flat = grp * n_dev + dev
    total = n_grp * n_dev

    def flat_device(index):
        return (index // n_dev, index % n_dev)

    north_id = flat_device((flat + 1) % total)
    south_id = flat_device((flat + total - 1) % total)

    def near_device(k):
        return (grp, ((k // 2) * nz + z) * 2 + k % 2)

    def far_device(k):
        return (grp, (x * nz + k) * 2 + core)

    barrier = pltpu.get_barrier_semaphore()
    for o in range(1, n_near):
        pl.semaphore_signal(barrier, 1, device_id=near_device((me + o) % n_near), device_id_type=MESH)
    for o in range(1, nz):
        pl.semaphore_signal(barrier, 1, device_id=far_device((z + o) % nz), device_id_type=MESH)
    pl.semaphore_signal(barrier, 1, device_id=north_id, device_id_type=MESH)
    pl.semaphore_signal(barrier, 1, device_id=south_id, device_id_type=MESH)

    dyn[...] = jnp.zeros_like(dyn)
    for f in range(3):
        for p in range(16):
            dyn[:, p, f * LANES : f * LANES + NLEV] = gcm_ref[f, :, p * NLEV : (p + 1) * NLEV]

    start = dyn[...].reshape(COLS, 3 * LANES)
    rounded = start.astype(BF16).astype(F32)
    lane = iota((COLS, LANES), 1)
    temper = jnp.where(lane < CZ, rounded[:, 0:LANES], 0.0)
    vapour = jnp.where(lane < CZ, rounded[:, LANES : 2 * LANES], 0.0)
    assigned = asg_ref[...].astype(F32)
    target = jnp.floor((assigned + 0.5) * (1.0 / SLOTS))
    slot = assigned - target * SLOTS + 1.0
    cost = cost_ref[...].astype(F32)
    sub = iota((LANES, COLS), 0)
    labels = jnp.where(sub == LANE_TARGET, target, 0.0)
    labels = jnp.where(sub == LANE_SLOT, slot, labels)
    labels = jnp.where(sub == LANE_COST, cost, labels).astype(BF16)
    eye = one_hot(iota((COLS, COLS), 0) == iota((COLS, COLS), 1))
    payload = temper + pltpu.roll(vapour, 64, 1) + dot_nt(eye, labels)
    got1[me] = payload.astype(BF16)

    wide_lane = iota((COLS, 3 * LANES), 1)
    keep = (wide_lane % LANES) >= CZ
    cloud = wide_lane >= 2 * LANES
    base[...] = jnp.where(keep, -0.5 * rounded, jnp.where(cloud, -rounded, 0.0))

    pl.semaphore_wait(barrier, n_near - 1 + nz - 1 + 2)

    def copy1(o):
        return pltpu.make_async_remote_copy(
            src_ref=got1.at[me],
            dst_ref=got1.at[me],
            send_sem=s1.at[o],
            recv_sem=r1.at[o],
            device_id=near_device((me + o) % n_near),
            device_id_type=MESH,
        )

    for o in range(1, n_near):
        copy1(o).start()

    def edge_copies(turn):
        return [
            pltpu.make_async_remote_copy(
                src_ref=edge_out.at[turn, side],
                dst_ref=edge_in.at[turn, side],
                send_sem=se.at[turn, side],
                recv_sem=re.at[turn, side],
                device_id=(south_id, north_id)[side],
                device_id_type=MESH,
            )
            for side in range(2)
        ]

    weights = edge_weights(nb_ref)

    def dynamics_send(turn):
        for e in range(2):
            local = dot_full(op_ref[e], dyn[e])
            near[16 * e : 16 * e + 16] = local
            edge_out[turn, 0, 4 * e : 4 * e + 4] = local[0:4]
            edge_out[turn, 1, 4 * e : 4 * e + 4] = local[12:16]
        for copy in edge_copies(turn):
            copy.start()

    def dynamics_finish(turn):
        for side, copy in enumerate(edge_copies(turn)):
            copy.wait_recv()
            near[32 + 8 * side : 40 + 8 * side] = edge_in[turn, side]
        dyn[...] = dyn[...] + dot_full(weights, near[...]).reshape(dyn.shape)

    dynamics_send(0)

    wide_row, wide_col = iota((256, 256), 0), iota((256, 256), 1)
    odd = wide_col & 1
    within = (wide_col & 127) >> 1
    regroup = []
    for first in (0, 1):
        side = odd ^ first
        moved = wide_row == 192 * side + within
        meaned = ((wide_row < 64) & (side == 0)) | ((wide_row >= 192) & (side == 1))
        regroup.append(jnp.where(wide_col < 128, jnp.where(moved, 1.0, 0.0), jnp.where(meaned, 1.0 / CX, 0.0)).astype(BF16))
    for f in range(2):
        for g in range(5):
            half_in[40 * f + 8 * g : 40 * f + 8 * g + 8, :] = crm_ref[8 * g : 8 * g + 8, f, :]

    def tile(t):
        return slice(t * LANES, (t + 1) * LANES)

    for j in range(HALF):
        pair = (j // 2, (j + HALF) // 2)
        left, right = pair if j % 2 == 0 else pair[::-1]
        both = jnp.concatenate([half_in[:, tile(left)], half_in[:, tile(right)]], axis=1)
        out = dot(both, regroup[j % 2])
        state_a[0:80, tile(j + 1)] = out[:, 0:LANES]
        drive[:, tile(j)] = out[:, LANES:]
    srow = iota((LANES, LANES), 0) & 63
    scol = iota((LANES, LANES), 1) & 1
    for j in range(HALF):
        spread[:, tile(j)] = one_hot(srow == j + HALF * scol)
    first_means = dot_nt(state_a[0:80, LANES : LANES + WIDE].astype(BF16), spread[...])

    for o in range(1, n_near):
        copy1(o).wait_recv()
    plane = got1[...].reshape(rows1, LANES)
    pick_row = iota((8, LANES), 0)
    pick_lane = iota((8, LANES), 1)
    picker = one_hot(pick_lane == LANE_TARGET + pick_row)
    owner = dot_nt(picker, plane)[0:1, :]
    zid = iota((nz, rows1), 0)
    mine = owner == (x * (2 * nz) + 2 * zid + core).astype(F32)
    hits = jnp.where(mine, 1.0, 0.0)
    before = one_hot(iota((rows1, rows1), 0) < iota((rows1, rows1), 1))
    earlier = dot(hits.astype(BF16), before)
    place = jnp.sum(hits * (zid.astype(F32) * cap2 + earlier + 1.0), axis=0, keepdims=True) - 1.0
    packer = jnp.where(iota((rows2, rows1), 0).astype(F32) == place, 1.0, 0.0)
    pack2[...] = dot(packer.astype(BF16), plane).astype(BF16).reshape(pack2.shape)

    def copy_far(o, src, dst, send, recv):
        to = (z + o) % nz
        return pltpu.make_async_remote_copy(
            src_ref=src.at[to],
            dst_ref=dst.at[z],
            send_sem=send.at[o],
            recv_sem=recv.at[o],
            device_id=far_device(to),
            device_id_type=MESH,
        )

    order = sorted(range(1, nz), key=lambda o: -min(o, nz - o))
    for o in order:
        copy_far(o, pack2, got2, s2, r2).start()
    got2[z] = pack2[z]
    unpacker = packer.T.astype(BF16)

    dynamics_finish(0)
    dynamics_send(1)

    for o in order:
        copy_far(o, pack2, got2, s2, r2).wait_recv()
    arrived = got2[...].reshape(rows2, LANES)
    slot_row = dot_nt(picker, arrived)[1:2, :]
    matcher = one_hot((iota((SLOTS, rows2), 0) + 1).astype(F32) == slot_row)
    forcing = dot(matcher, arrived)
    slot_col = arrived[:, LANE_SLOT : LANE_SLOT + 1].astype(F32)
    matcher_t = one_hot((iota((rows2, LANES), 1) + 1).astype(F32) == slot_col)
    slot_lane = iota((SLOTS, LANES), 1)
    stacked = jnp.concatenate(
        [jnp.where(slot_lane < 64, forcing, 0.0), jnp.where(slot_lane < 64, 0.0, forcing)], axis=0
    ).astype(BF16)
    drive[...] = 0.3 * (dot(stacked, spread[...]) - drive[...])
    near_counts = jnp.broadcast_to(forcing[:, LANE_COST : LANE_COST + 1], (SLOTS, LANES))
    tend[...] = jnp.zeros_like(tend)
    tend[0:SLOTS, 0:LANES] = near_counts

    def slot_group(g, carry):
        top = pl.ds(pl.multiple_of(8 * g, 8), 8)
        low = pl.ds(pl.multiple_of(8 * g + 40, 8), 8)
        last = pl.ds(pl.multiple_of(8 * g + 80, 8), 8)
        steps = tend[top, 0:LANES]
        is_odd = (iota((8, LANES), 1) & 1) == 1
        slope = jnp.where(is_odd, 0.4, 0.0)
        source, sink = state_a, state_b
        for n in range(NSUB):
            active = steps > n + 0.5
            for rows in (top, low):
                first, final = source[rows, tile(1)], source[rows, tile(HALF)]
                source[rows, tile(0)] = jnp.where(is_odd, pltpu.roll(final, 1, 1), first)
                source[rows, tile(HALF + 1)] = jnp.where(is_odd, final, pltpu.roll(first, LANES - 1, 1))
            for j in range(HALF):
                now, mixed = [], []
                for rows in (top, low):
                    own = source[rows, tile(j + 1)]
                    around = (
                        own
                        + source[rows, tile(j)]
                        + source[rows, tile(j + 2)]
                        + pltpu.roll(own, 2, 1)
                        + pltpu.roll(own, LANES - 2, 1)
                    )
                    now.append(own)
                    mixed.append(0.2 * around + drive[rows, tile(j)])
                sat = ((0.5 - 0.8 * j / CZ) - slope) + 0.2 * mixed[0]
                moved = 0.5 * jnp.maximum(mixed[1] - sat, 0.0)
                t_new = jnp.where(active, mixed[0] + moved, now[0])
                w_new = jnp.where(active, mixed[1] - moved, now[1])
                sink[top, tile(j + 1)] = t_new
                sink[low, tile(j + 1)] = w_new
                if n == NSUB - 1:
                    sat = ((0.5 - 0.8 * j / CZ) - slope) + 0.2 * t_new
                    sink[last, tile(j + 1)] = jnp.maximum(w_new - sat, 0.0)
            source, sink = sink, source
        return carry

    lax.fori_loop(0, SLOTS // 8, slot_group, 0)

    final = state_a[:, LANES : LANES + WIDE].astype(BF16)
    means = dot_nt(final, spread[...])
    change = (means[0:80] - first_means) * (1.0 / CX)
    tend[0:SLOTS, 0:LANES] = jnp.where(slot_lane < 64, change[0:40], change[40:80])
    tend[0:SLOTS, LANES:] = means[80:120] * (1.0 / CX)
    pack3[...] = dot(matcher_t, tend[...].astype(BF16)).astype(BF16).reshape(pack3.shape)
    for o in order:
        copy_far(o, pack3, got3, s3, r3).start()
    got3[z] = pack3[z]

    dynamics_finish(1)
    dynamics_send(2)

    back_row, back_col = iota((256, LANES), 0), iota((256, LANES), 1)
    put = 2 * (back_col & 63) + 128 * (back_col >> 6)
    both_low = one_hot(back_row == put)
    both_high = one_hot(back_row == put + 1)
    split = one_hot(back_row == put + (back_col >> 6))
    for t in range(HALF):
        if t < HALF // 2:
            pair, matrix = (2 * t, 2 * t + 1), both_low
        elif t == HALF // 2:
            pair, matrix = (2 * t, 0), split
        else:
            pair, matrix = (2 * t - HALF, 2 * t - HALF + 1), both_high
        both = jnp.concatenate([state_a[0:80, tile(k + 1)] for k in pair], axis=1).astype(BF16)
        half_in[:, tile(t)] = dot(both, matrix).astype(BF16)
    for f in range(2):
        for g in range(5):
            cout_ref[8 * g : 8 * g + 8, f, :] = half_in[40 * f + 8 * g : 40 * f + 8 * g + 8, :]

    for o in order:
        copy_far(o, pack3, got3, s3, r3).wait_recv()
    pack4[...] = dot(unpacker, got3[...].reshape(rows2, 256)).astype(BF16).reshape(pack4.shape)

    def copy4(o):
        to = (me + o) % n_near
        return pltpu.make_async_remote_copy(
            src_ref=pack4.at[to],
            dst_ref=got4.at[me],
            send_sem=s4.at[o],
            recv_sem=r4.at[o],
            device_id=near_device(to),
            device_id_type=MESH,
        )

    for o in range(1, n_near):
        copy4(o).start()
    got4[me] = pack4[me]

    dynamics_finish(2)

    for o in range(1, n_near):
        copy4(o).wait_recv()
    col = got4[0].astype(F32)
    for k in range(1, n_near):
        col = col + got4[k].astype(F32)
    temper = jnp.where(lane < CZ, col[:, 0:LANES], 0.0)
    vapour = jnp.where(lane < CZ, pltpu.roll(col[:, 0:LANES], 64, 1), 0.0)
    cloud = jnp.where(lane < CZ, col[:, LANES:], 0.0)
    gained = jnp.concatenate([temper, vapour, cloud], axis=1) + base[...]
    result = dyn[...] + gained.astype(BF16).astype(F32).reshape(dyn.shape)
    for f in range(3):
        for p in range(16):
            gout_ref[f, :, p * NLEV : (p + 1) * NLEV] = result[:, p, f * LANES : f * LANES + NLEV]

    for o in range(1, n_near):
        copy1(o).wait_send()
        copy4(o).wait_send()
    for o in order:
        copy_far(o, pack2, got2, s2, r2).wait_send()
        copy_far(o, pack3, got3, s3, r3).wait_send()
    for turn in range(NDYN):
        for copy in edge_copies(turn):
            copy.wait_send()


def body(dims, gcm_state, element_op, neighbours, crm_state, assignment, column_cost):
    n_grp, nx, nz, cap = dims
    n_near = 2 * nx
    cap2 = cap * n_near
    vmem = pl.BlockSpec(memory_space=pltpu.VMEM)
    dma = pltpu.SemaphoreType.DMA
    gcm = gcm_state.transpose(1, 0, 2)
    gout, cout = pl.pallas_call(
        functools.partial(kernel, dims),
        out_shape=(
            jax.ShapeDtypeStruct(gcm.shape, F32),
            jax.ShapeDtypeStruct(crm_state.shape, BF16),
        ),
        in_specs=[vmem, vmem, pl.BlockSpec(memory_space=pltpu.SMEM), vmem, vmem, vmem],
        out_specs=(vmem, vmem),
        scratch_shapes=[
            pltpu.VMEM((2, 16, 3 * LANES), F32),
            pltpu.VMEM((COLS, 3 * LANES), F32),
            pltpu.VMEM((48, 3 * LANES), F32),
            pltpu.VMEM((NDYN, 2, 8, 3 * LANES), F32),
            pltpu.VMEM((NDYN, 2, 8, 3 * LANES), F32),
            pltpu.VMEM((n_near, COLS, LANES), BF16),
            pltpu.VMEM((nz, cap2, LANES), BF16),
            pltpu.VMEM((nz, cap2, LANES), BF16),
            pltpu.VMEM((nz, cap2, 2 * LANES), BF16),
            pltpu.VMEM((nz, cap2, 2 * LANES), BF16),
            pltpu.VMEM((n_near, COLS, 2 * LANES), BF16),
            pltpu.VMEM((n_near, COLS, 2 * LANES), BF16),
            pltpu.VMEM((120, WIDE + 2 * LANES), F32),
            pltpu.VMEM((120, WIDE + 2 * LANES), F32),
            pltpu.VMEM((80, WIDE), F32),
            pltpu.VMEM((80, WIDE), BF16),
            pltpu.VMEM((LANES, WIDE), BF16),
            pltpu.VMEM((LANES, 2 * LANES), F32),
            dma((n_near,)),
            dma((n_near,)),
            dma((nz,)),
            dma((nz,)),
            dma((nz,)),
            dma((nz,)),
            dma((n_near,)),
            dma((n_near,)),
            dma((NDYN, 2)),
            dma((NDYN, 2)),
        ],
        compiler_params=pltpu.CompilerParams(
            collective_id=0, has_side_effects=True, vmem_limit_bytes=40 * 2**20
        ),
        name="physics_and_dynamics",
    )(gcm, element_op, neighbours, crm_state, assignment.reshape(1, -1), column_cost.reshape(1, -1))
    return gout.transpose(1, 0, 2), cout


def solution(mesh):
    n_grp, n_dev = mesh.shape["grp"], mesh.shape["dev"]
    nz = 16 if n_dev % 32 == 0 else n_dev // 4
    nx = n_dev // (2 * nz)
    cap = 2 * ((COLS + n_dev - 1) // n_dev)
    in_specs = (
        P(("grp", "dev"), None, None),
        P(("grp", "dev"), None, None),
        P(("grp", "dev"), None),
        P(("grp", "dev"), None, None),
        P(("grp", "dev")),
        P(("grp", "dev")),
    )
    out_specs = (P(("grp", "dev"), None, None), P(("grp", "dev"), None, None))
    return jax.shard_map(
        functools.partial(body, (n_grp, nx, nz, cap)),
        mesh=mesh,
        in_specs=in_specs,
        out_specs=out_specs,
        check_vma=False,
    )
```

time: 182 us -> 61.2 us (0.34)
  starting transfers between devices: 68.6 us -> 0 us
  Pallas kernels: 0 us -> 55.6 us
  local copies, waits for them, and re-layouts: 53.2 us -> 4.63 us
  other arithmetic: 30.5 us -> 0 us
  waiting for transfers between devices: 25.1 us -> 0 us
  matrix products: 2.26 us -> 0 us
    pallas_call x0 -> x1, Pallas kernels: none -> 55.6 us  [body(): pl.pallas_call(functools.partial(kernel, dims), out_shape=(jax.ShapeDtype...]
    ppermute x6 -> x0, starting transfers between devices: 40.8 us -> none  [the longest x3 33.5 us: with_halo(): after = lax.ppermute(leading, axis, down)]
    all_to_all x3 -> x0, starting transfers between devices: 27.8 us -> none  [the longest x1 13.5 us: body(): lax.all_to_all(packed_labels.reshape(peer_count, capacity, 2), 'dev', spl...]
    all_to_all x3 -> x0, waiting for transfers between devices: 25.1 us -> none  [the longest x1 15.4 us: body(): lax.all_to_all(back_rows.reshape(peer_count, capacity, 3 * sent_levels),...]
    gather x28 -> x0, local copies, waits for them, and re-layouts: 19.7 us -> none  [the longest x3 2.67 us: body(): below_north[south_ids[west_ids]][:, :, 3]]
    reshape x16 -> x0, local copies, waits for them, and re-layouts: 11.6 us -> none  [the longest x2 5.07 us: level_means(): return jnp.mean(flat_fields.reshape(shape[:-1] + (CZ, CX)), axis=-1)]
    add x23 -> x0, other arithmetic: 10.3 us -> none  [the longest x4 7.84 us: cloud_model(): fields + drive_flat + HORIZONTAL_MIX * across + VERTICAL_MIX * vertical]
    slice x24 -> x0, local copies, waits for them, and re-layouts: 9.96 us -> none  [the longest x8 3.87 us: cloud_model(): jnp.roll(fields, CX - 1, axis=-1)]
  transfers between devices with their start and end apart: 9 -> 0, of which waited for: 2 -> 0; matrix products, arithmetic and copies ran while one was open for 23% -> 0% of each run, Pallas kernels for 0% -> 0%
where the time goes in v1:
time: 61.2 us; the launch traced here: 60.9 us
  Pallas kernels  55.6 us (91%)
  local copies, waits for them, and re-layouts  4.63 us (8%)
  between operations  0.67 us (1%)
    pallas_call x1, Pallas kernels, body(): pl.pallas_call(functools.partial(kernel, dims), out_shape=(jax.ShapeDtype...  55.6 us
    unnamed x14, local copies, waits for them, and re-layouts  4.63 us

profile of v1, /device:TPU:1, one launch (start us, length us, event | category | flops | bytes accessed | tf_op | source)
XLA Modules:
  0.0 60.9 jit_solution(12886342757347455985)
XLA Ops:
  0.6 0.0 copy-start.5
  0.6 0.0 copy-start.3
  0.7 0.0 copy-start.4
  0.7 0.6 %copy-done.5 = s32[32]{0:T(128)S(1)} copy-done((s32[32]{0:T(128)S(1)}, s32[32]{0:T(128)}, u32[]{:S(2)}) %copy-start.5) | copy-done | bytes 152
  1.3 0.0 copy-done.3
  1.3 0.0 copy-done.4
  1.3 0.0 copy-start
  1.3 1.1 %copy-done = bf16[40,2,3712]{2,1,0:T(2,128)(2,1)S(1)} copy-done((bf16[40,2,3712]{2,1,0:T(2,128)(2,1)S(1)}, bf16[40,2,3712]{2,1,0:T(2,128)(2,1)}, u32[]{:S(2)}) %copy-start) | copy-done | bytes 593944
  2.4 0.0 copy-start.1
  2.4 0.7 %copy-done.1 = f32[2,3,1152]{2,0,1:T(2,128)S(1)} copy-done((f32[2,3,1152]{2,0,1:T(2,128)S(1)}, f32[2,3,1152]{2,0,1:T(2,128)}, u32[]{:S(2)}) %copy-start.1) | copy-done | bytes 27672
  3.1 0.0 copy-start.2
  3.1 0.7 %copy-done.2 = f32[2,16,16]{2,1,0:T(8,128)S(1)} copy-done((f32[2,16,16]{2,1,0:T(8,128)S(1)}, f32[2,16,16]{2,1,0:T(8,128)}, u32[]{:S(2)}) %copy-start.2) | copy-done | bytes 2072
  3.9 55.6 %physics_and_dynamics.1 = (f32[3,2,1152]{2,1,0:T(2,128)S(1)}, bf16[40,2,3712]{2,1,0:T(2,128)(2,1)S(1)}) custom-call(f32[3,2,1152]{2,1,0:T(2,128)S(1)} %bitcast.5, f32[2,16,16]{2,1,0:T(8,128)S(1)} %copy-done.2, s32[2,4]{1,0:T(2,128)S(1)} %copy-done.3, bf16[40,2,3712]{2,1,0:T(2,128)(2,1)S(1)} %copy-done, s32[1,32]{1,0:T(1,128)S(1)} %bitcast.6, s32[1,32]{1,0:T(1,128)S(1)} %bitcast.7), custom_call_target="tpu_custom_call" | custom-call | tf_op jit(solution)/shard_map/physics_and_dynamics/pallas_call | solution.py:430
  59.5 0.6 %copy.10 = f32[2,3,1152]{2,0,1:T(2,128)} copy(f32[2,3,1152]{2,0,1:T(2,128)S(1)} %bitcast.4) | data formatting | bytes 55296
  60.1 0.8 %copy.11 = bf16[40,2,3712]{2,1,0:T(2,128)(2,1)} copy(bf16[40,2,3712]{2,1,0:T(2,128)(2,1)S(1)} %get-tuple-element.9) | data formatting | bytes 1187840
Async XLA Ops:
  0.6 0.7 %copy-start.5 = (s32[32]{0:T(128)S(1)}, s32[32]{0:T(128)}, u32[]{:S(2)}) copy-start(s32[32]{0:T(128)} %param.11) | copy-start | bytes 388
  0.6 0.7 %copy-start.3 = (s32[2,4]{1,0:T(2,128)S(1)}, s32[2,4]{1,0:T(2,128)}, u32[]{:S(2)}) copy-start(s32[2,4]{1,0:T(2,128)} %nb_ref.1) | copy-start | bytes 100
  0.7 0.7 %copy-start.4 = (s32[32]{0:T(128)S(1)}, s32[32]{0:T(128)}, u32[]{:S(2)}) copy-start(s32[32]{0:T(128)} %param.10) | copy-start | bytes 388
  1.3 1.1 %copy-start = (bf16[40,2,3712]{2,1,0:T(2,128)(2,1)S(1)}, bf16[40,2,3712]{2,1,0:T(2,128)(2,1)}, u32[]{:S(2)}) copy-start(bf16[40,2,3712]{2,1,0:T(2,128)(2,1)} %crm_ref.1) | copy-start | bytes 1781764
  2.4 0.7 %copy-start.1 = (f32[2,3,1152]{2,0,1:T(2,128)S(1)}, f32[2,3,1152]{2,0,1:T(2,128)}, u32[]{:S(2)}) copy-start(f32[2,3,1152]{2,0,1:T(2,128)} %param.6) | copy-start | bytes 82948
  3.1 0.7 %copy-start.2 = (f32[2,16,16]{2,1,0:T(8,128)S(1)}, f32[2,16,16]{2,1,0:T(8,128)}, u32[]{:S(2)}) copy-start(f32[2,16,16]{2,1,0:T(8,128)} %op_ref.1) | copy-start | bytes 6148

commit v2 on v1

--- a/solution.py
+++ b/solution.py
@@ -54,7 +54,7 @@
     j, i = p // 4, p % 4
 
     def pick(direction, which):
-        first, second = nb_ref[0, direction] % 2, nb_ref[1, direction] % 2
+        first, second = nb_ref[0:1, direction : direction + 1] & 1, nb_ref[1:2, direction : direction + 1] & 1
         return jnp.where(which == 0, first, second)
 
     east, north, west, south = (pick(d, e) for d in range(4))
@@ -75,14 +75,20 @@
 
 def kernel(
     dims,
+    gcm_hbm,
+    op_hbm,
+    nb_hbm,
+    crm_hbm,
+    asg_hbm,
+    cost_hbm,
+    gout_ref,
+    cout_ref,
     gcm_ref,
     op_ref,
     nb_ref,
     crm_ref,
     asg_ref,
     cost_ref,
-    gout_ref,
-    cout_ref,
     dyn,
     base,
     near,
@@ -111,6 +117,7 @@
     r4,
     se,
     re,
+    si,
 ):
     n_grp, nx, nz, cap = dims
     n_near = nx * 2
@@ -146,7 +153,21 @@
     pl.semaphore_signal(barrier, 1, device_id=north_id, device_id_type=MESH)
     pl.semaphore_signal(barrier, 1, device_id=south_id, device_id_type=MESH)
 
+    loads = {}
+    pairs = (
+        ("gcm", gcm_hbm, gcm_ref),
+        ("asg", asg_hbm, asg_ref),
+        ("cost", cost_hbm, cost_ref),
+        ("op", op_hbm, op_ref),
+        ("nb", nb_hbm, nb_ref),
+        ("crm", crm_hbm, crm_ref),
+    )
+    for number, (which, src, dst) in enumerate(pairs):
+        loads[which] = pltpu.make_async_copy(src, dst, si.at[number])
+        loads[which].start()
+
     dyn[...] = jnp.zeros_like(dyn)
+    loads["gcm"].wait()
     for f in range(3):
         for p in range(16):
             dyn[:, p, f * LANES : f * LANES + NLEV] = gcm_ref[f, :, p * NLEV : (p + 1) * NLEV]
@@ -156,6 +177,8 @@
     lane = iota((COLS, LANES), 1)
     temper = jnp.where(lane < CZ, rounded[:, 0:LANES], 0.0)
     vapour = jnp.where(lane < CZ, rounded[:, LANES : 2 * LANES], 0.0)
+    loads["asg"].wait()
+    loads["cost"].wait()
     assigned = asg_ref[...].astype(F32)
     target = jnp.floor((assigned + 0.5) * (1.0 / SLOTS))
     slot = assigned - target * SLOTS + 1.0
@@ -201,6 +224,8 @@
             for side in range(2)
         ]
 
+    loads["nb"].wait()
+    loads["op"].wait()
     weights = edge_weights(nb_ref)
 
     def dynamics_send(turn):
@@ -229,6 +254,7 @@
         moved = wide_row == 192 * side + within
         meaned = ((wide_row < 64) & (side == 0)) | ((wide_row >= 192) & (side == 1))
         regroup.append(jnp.where(wide_col < 128, jnp.where(moved, 1.0, 0.0), jnp.where(meaned, 1.0 / CX, 0.0)).astype(BF16))
+    loads["crm"].wait()
     for f in range(2):
         for g in range(5):
             half_in[40 * f + 8 * g : 40 * f + 8 * g + 8, :] = crm_ref[8 * g : 8 * g + 8, f, :]
@@ -302,10 +328,8 @@
     tend[...] = jnp.zeros_like(tend)
     tend[0:SLOTS, 0:LANES] = near_counts
 
-    def slot_group(g, carry):
-        top = pl.ds(pl.multiple_of(8 * g, 8), 8)
-        low = pl.ds(pl.multiple_of(8 * g + 40, 8), 8)
-        last = pl.ds(pl.multiple_of(8 * g + 80, 8), 8)
+    def slot_group(g):
+        top, low, last = (slice(8 * g + 40 * k, 8 * g + 40 * k + 8) for k in range(3))
         steps = tend[top, 0:LANES]
         is_odd = (iota((8, LANES), 1) & 1) == 1
         slope = jnp.where(is_odd, 0.4, 0.0)
@@ -339,9 +363,9 @@
                     sat = ((0.5 - 0.8 * j / CZ) - slope) + 0.2 * t_new
                     sink[last, tile(j + 1)] = jnp.maximum(w_new - sat, 0.0)
             source, sink = sink, source
-        return carry
-
-    lax.fori_loop(0, SLOTS // 8, slot_group, 0)
+
+    for g in range(SLOTS // 8):
+        slot_group(g)
 
     final = state_a[:, LANES : LANES + WIDE].astype(BF16)
     means = dot_nt(final, spread[...])
@@ -433,9 +457,15 @@
             jax.ShapeDtypeStruct(gcm.shape, F32),
             jax.ShapeDtypeStruct(crm_state.shape, BF16),
         ),
-        in_specs=[vmem, vmem, pl.BlockSpec(memory_space=pltpu.SMEM), vmem, vmem, vmem],
+        in_specs=[pl.BlockSpec(memory_space=pltpu.HBM)] * 6,
         out_specs=(vmem, vmem),
         scratch_shapes=[
+            pltpu.VMEM(gcm.shape, F32),
+            pltpu.VMEM(element_op.shape, F32),
+            pltpu.VMEM(neighbours.shape, jnp.int32),
+            pltpu.VMEM(crm_state.shape, BF16),
+            pltpu.VMEM((1, COLS), jnp.int32),
+            pltpu.VMEM((1, COLS), jnp.int32),
             pltpu.VMEM((2, 16, 3 * LANES), F32),
             pltpu.VMEM((COLS, 3 * LANES), F32),
             pltpu.VMEM((48, 3 * LANES), F32),
@@ -464,9 +494,10 @@
             dma((n_near,)),
             dma((NDYN, 2)),
             dma((NDYN, 2)),
+            dma((6,)),
         ],
         compiler_params=pltpu.CompilerParams(
-            collective_id=0, has_side_effects=True, vmem_limit_bytes=40 * 2**20
+            collective_id=0, has_side_effects=True, vmem_limit_bytes=65000 * 1024
         ),
         name="physics_and_dynamics",
     )(gcm, element_op, neighbours, crm_state, assignment.reshape(1, -1), column_cost.reshape(1, -1))

time: 61.2 us -> 56.5 us (0.923)
  Pallas kernels: 55.6 us -> 52 us
  local copies, waits for them, and re-layouts: 4.63 us -> 3.65 us
    pallas_call x1, Pallas kernels: 55.6 us -> 52 us  [body(): pl.pallas_call(functools.partial(kernel, dims), out_shape=(jax.ShapeDtype...]
    unnamed x14 -> x2, local copies, waits for them, and re-layouts: 4.63 us -> 3.65 us
where the time goes in v2:
time: 56.5 us; the launch traced here: 56.3 us
  Pallas kernels  52 us (92%)
  local copies, waits for them, and re-layouts  3.65 us (6%)
  between operations  0.64 us (1%)
    pallas_call x1, Pallas kernels, body(): pl.pallas_call(functools.partial(kernel, dims), out_shape=(jax.ShapeDtype...  52 us
    unnamed x2, local copies, waits for them, and re-layouts  3.65 us

profile of v2, /device:TPU:1, one launch (start us, length us, event | category | flops | bytes accessed | tf_op | source)
XLA Modules:
  0.0 56.3 jit_solution(15927202590728875796)
XLA Ops:
  0.6 52.0 %physics_and_dynamics.1 = (f32[3,2,1152]{2,1,0:T(2,128)}, bf16[40,2,3712]{2,1,0:T(2,128)(2,1)}) custom-call(f32[3,2,1152]{2,1,0:T(2,128)} %bitcast.5, f32[2,16,16]{2,1,0:T(8,128)} %op_hbm.1, s32[2,4]{1,0:T(2,128)} %nb_hbm.1, bf16[40,2,3712]{2,1,0:T(2,128)(2,1)} %crm_hbm.1, s32[1,32]{1,0:T(1,128)} %bitcast.6, s32[1,32]{1,0:T(1,128)} %bitcast.7), custom_call_target="tpu_custom_call" | custom-call | tf_op jit(solution)/shard_map/physics_and_dynamics/pallas_call | solution.py:454
  52.6 1.4 %copy.10 = f32[2,3,1152]{2,0,1:T(2,128)} copy(f32[2,3,1152]{2,0,1:T(2,128)} %bitcast.4) | data formatting | bytes 55296
  54.0 2.3 %copy.11 = bf16[40,2,3712]{2,1,0:T(2,128)(2,1)} copy(bf16[40,2,3712]{2,1,0:T(2,128)(2,1)} %get-tuple-element.9) | data formatting | bytes 1187840

commit v3 on v2

--- a/solution.py
+++ b/solution.py
@@ -81,6 +81,8 @@
     crm_hbm,
     asg_hbm,
     cost_hbm,
+    gout_hbm,
+    cout_hbm,
     gout_ref,
     cout_ref,
     gcm_ref,
@@ -118,6 +120,8 @@
     se,
     re,
     si,
+    plane_in,
+    line_in,
 ):
     n_grp, nx, nz, cap = dims
     n_near = nx * 2
@@ -145,13 +149,22 @@
     def far_device(k):
         return (grp, (x * nz + k) * 2 + core)
 
+    def far_line(k):
+        return (grp, (x * nz + k % nz) * 2 + 1)
+
     barrier = pltpu.get_barrier_semaphore()
-    for o in range(1, n_near):
-        pl.semaphore_signal(barrier, 1, device_id=near_device((me + o) % n_near), device_id_type=MESH)
+
+    def announce(semaphore, device):
+        pl.semaphore_signal(semaphore, 1, device_id=device, device_id_type=MESH)
+
+    sibling = near_device(2 * x + 1 - core)
     for o in range(1, nz):
-        pl.semaphore_signal(barrier, 1, device_id=far_device((z + o) % nz), device_id_type=MESH)
-    pl.semaphore_signal(barrier, 1, device_id=north_id, device_id_type=MESH)
-    pl.semaphore_signal(barrier, 1, device_id=south_id, device_id_type=MESH)
+        announce(barrier, far_line(z + o))
+    for o in range(1, nx):
+        announce(barrier, near_device(2 * ((x + o) % nx)))
+    announce(barrier, sibling)
+    announce(barrier, north_id)
+    announce(barrier, south_id)
 
     loads = {}
     pairs = (
@@ -196,7 +209,14 @@
     cloud = wide_lane >= 2 * LANES
     base[...] = jnp.where(keep, -0.5 * rounded, jnp.where(cloud, -rounded, 0.0))
 
-    pl.semaphore_wait(barrier, n_near - 1 + nz - 1 + 2)
+    @pl.when(core == 0)
+    def _():
+        pl.semaphore_wait(barrier, 2 * nx - 1 + 2)
+        announce(plane_in, sibling)
+
+    @pl.when(core == 1)
+    def _():
+        pl.semaphore_wait(plane_in, 1)
 
     def copy1(o):
         return pltpu.make_async_remote_copy(
@@ -243,7 +263,6 @@
             near[32 + 8 * side : 40 + 8 * side] = edge_in[turn, side]
         dyn[...] = dyn[...] + dot_full(weights, near[...]).reshape(dyn.shape)
 
-    dynamics_send(0)
 
     wide_row, wide_col = iota((256, 256), 0), iota((256, 256), 1)
     odd = wide_col & 1
@@ -274,6 +293,13 @@
     for j in range(HALF):
         spread[:, tile(j)] = one_hot(srow == j + HALF * scol)
     first_means = dot_nt(state_a[0:80, LANES : LANES + WIDE].astype(BF16), spread[...])
+
+    @pl.when(core == 1)
+    def _():
+        pl.semaphore_wait(barrier, 2 * nz - 1 + 2)
+        announce(line_in, sibling)
+
+    dynamics_send(0)
 
     for o in range(1, n_near):
         copy1(o).wait_recv()
@@ -303,6 +329,10 @@
         )
 
     order = sorted(range(1, nz), key=lambda o: -min(o, nz - o))
+    @pl.when(core == 0)
+    def _():
+        pl.semaphore_wait(line_in, 1)
+
     for o in order:
         copy_far(o, pack2, got2, s2, r2).start()
     got2[z] = pack2[z]
@@ -397,6 +427,8 @@
     for f in range(2):
         for g in range(5):
             cout_ref[8 * g : 8 * g + 8, f, :] = half_in[40 * f + 8 * g : 40 * f + 8 * g + 8, :]
+    store_cout = pltpu.make_async_copy(cout_ref, cout_hbm, si.at[6])
+    store_cout.start()
 
     for o in order:
         copy_far(o, pack3, got3, s3, r3).wait_recv()
@@ -432,6 +464,8 @@
     for f in range(3):
         for p in range(16):
             gout_ref[f, :, p * NLEV : (p + 1) * NLEV] = result[:, p, f * LANES : f * LANES + NLEV]
+    store_gout = pltpu.make_async_copy(gout_ref, gout_hbm, si.at[7])
+    store_gout.start()
 
     for o in range(1, n_near):
         copy1(o).wait_send()
@@ -442,13 +476,34 @@
     for turn in range(NDYN):
         for copy in edge_copies(turn):
             copy.wait_send()
+    store_cout.wait()
+    store_gout.wait()
+
+
+PARTS = 2
+
+
+def hand_over(gout_ref, cout_ref, gout_final, cout_final, gout_mid, cout_mid, sem_in, sem_out):
+    chunk = SLOTS // PARTS
+    parts = [pl.ds(chunk * g, chunk) for g in range(PARTS)]
+    fetch = [pltpu.make_async_copy(cout_ref.at[r], cout_mid.at[r], sem_in.at[g]) for g, r in enumerate(parts)]
+    store = [pltpu.make_async_copy(cout_mid.at[r], cout_final.at[r], sem_out.at[g]) for g, r in enumerate(parts)]
+    fetch.append(pltpu.make_async_copy(gout_ref, gout_mid, sem_in.at[PARTS]))
+    store.append(pltpu.make_async_copy(gout_mid, gout_final, sem_out.at[PARTS]))
+    for copy in fetch:
+        copy.start()
+    for first, second in zip(fetch, store):
+        first.wait()
+        second.start()
+    for copy in store:
+        copy.wait()
 
 
 def body(dims, gcm_state, element_op, neighbours, crm_state, assignment, column_cost):
     n_grp, nx, nz, cap = dims
     n_near = 2 * nx
     cap2 = cap * n_near
-    vmem = pl.BlockSpec(memory_space=pltpu.VMEM)
+    hbm = pl.BlockSpec(memory_space=pltpu.HBM)
     dma = pltpu.SemaphoreType.DMA
     gcm = gcm_state.transpose(1, 0, 2)
     gout, cout = pl.pallas_call(
@@ -458,8 +513,10 @@
             jax.ShapeDtypeStruct(crm_state.shape, BF16),
         ),
         in_specs=[pl.BlockSpec(memory_space=pltpu.HBM)] * 6,
-        out_specs=(vmem, vmem),
+        out_specs=(hbm, hbm),
         scratch_shapes=[
+            pltpu.VMEM(gcm.shape, F32),
+            pltpu.VMEM(crm_state.shape, BF16),
             pltpu.VMEM(gcm.shape, F32),
             pltpu.VMEM(element_op.shape, F32),
             pltpu.VMEM(neighbours.shape, jnp.int32),
@@ -494,13 +551,33 @@
             dma((n_near,)),
             dma((NDYN, 2)),
             dma((NDYN, 2)),
-            dma((6,)),
+            dma((8,)),
+            pltpu.SemaphoreType.REGULAR,
+            pltpu.SemaphoreType.REGULAR,
         ],
         compiler_params=pltpu.CompilerParams(
             collective_id=0, has_side_effects=True, vmem_limit_bytes=65000 * 1024
         ),
         name="physics_and_dynamics",
     )(gcm, element_op, neighbours, crm_state, assignment.reshape(1, -1), column_cost.reshape(1, -1))
+    vmem_limit = pltpu.CompilerParams(vmem_limit_bytes=65000 * 1024)
+    gout, cout = pl.pallas_call(
+        hand_over,
+        out_shape=(
+            jax.ShapeDtypeStruct(gcm.shape, F32),
+            jax.ShapeDtypeStruct(crm_state.shape, BF16),
+        ),
+        in_specs=[hbm] * 2,
+        out_specs=(hbm, hbm),
+        scratch_shapes=[
+            pltpu.VMEM(gcm.shape, F32),
+            pltpu.VMEM(crm_state.shape, BF16),
+            dma((1 + PARTS,)),
+            dma((1 + PARTS,)),
+        ],
+        compiler_params=vmem_limit,
+        name="hand_over",
+    )(gout, cout)
     return gout.transpose(1, 0, 2), cout
 
 

time: 56.5 us -> 54 us (0.956)
  local copies, waits for them, and re-layouts: 3.65 us -> 0 us
  Pallas kernels: 52 us -> 53.2 us
    unnamed x2 -> x0, local copies, waits for them, and re-layouts: 3.65 us -> none
    pallas_call x0 -> x1, Pallas kernels: none -> 1.83 us  [body(): pl.pallas_call(hand_over, out_shape=(jax.ShapeDtypeStruct(gcm.shape, F32)...]
    pallas_call x1, Pallas kernels: 52 us -> 51.4 us  [body(): pl.pallas_call(functools.partial(kernel, dims), out_shape=(jax.ShapeDtype...]
where the time goes in v3:
time: 54 us; the launch traced here: 53.8 us
  Pallas kernels  53.2 us (99%)
  between operations  0.64 us (1%)
    pallas_call x1, Pallas kernels, body(): pl.pallas_call(functools.partial(kernel, dims), out_shape=(jax.ShapeDtype...  51.4 us
    pallas_call x1, Pallas kernels, body(): pl.pallas_call(hand_over, out_shape=(jax.ShapeDtypeStruct(gcm.shape, F32)...  1.83 us

profile of v3, /device:TPU:1, one launch (start us, length us, event | category | flops | bytes accessed | tf_op | source)
XLA Modules:
  0.0 53.8 jit_solution(16691009319882959431)
XLA Ops:
  0.6 51.4 %physics_and_dynamics.1 = (f32[3,2,1152]{2,1,0:T(2,128)}, bf16[40,2,3712]{2,1,0:T(2,128)(2,1)}) custom-call(f32[3,2,1152]{2,1,0:T(2,128)} %bitcast.4, f32[2,16,16]{2,1,0:T(8,128)} %op_hbm.1, s32[2,4]{1,0:T(2,128)} %nb_hbm.1, bf16[40,2,3712]{2,1,0:T(2,128)(2,1)} %crm_hbm.1, s32[1,32]{1,0:T(1,128)} %bitcast.5, s32[1,32]{1,0:T(1,128)} %bitcast.6), custom_call_target="tpu_custom_call" | custom-call | tf_op jit(solution)/shard_map/physics_and_dynamics/pallas_call | solution.py:509
  52.0 1.8 %hand_over.1 = (f32[3,2,1152]{2,1,0:T(2,128)}, bf16[40,2,3712]{2,1,0:T(2,128)(2,1)}) custom-call(f32[3,2,1152]{2,1,0:T(2,128)} %get-tuple-element.6.gout_ref, bf16[40,2,3712]{2,1,0:T(2,128)(2,1)} %get-tuple-element.7.cout_ref), custom_call_target="tpu_custom_call" | custom-call | tf_op jit(solution)/shard_map/hand_over/pallas_call | solution.py:564

commit v4 on v3

--- a/solution.py
+++ b/solution.py
@@ -22,9 +22,10 @@
 BF16 = jnp.bfloat16
 F32 = jnp.float32
 
-LANE_TARGET = 58
-LANE_SLOT = 59
-LANE_COST = 60
+LANE_PLACE = 58
+LANE_CLASS = 59
+LANE_SLOT = 60
+LANE_COST = 61
 
 
 def iota(shape, axis):
@@ -106,6 +107,7 @@
     state_a,
     state_b,
     drive,
+    forced,
     half_in,
     spread,
     tend,
@@ -163,8 +165,7 @@
     for o in range(1, nx):
         announce(barrier, near_device(2 * ((x + o) % nx)))
     announce(barrier, sibling)
-    announce(barrier, north_id)
-    announce(barrier, south_id)
+    announce(barrier, flat_device((flat + jnp.where(core == 0, total - 1, 2)) % total))
 
     loads = {}
     pairs = (
@@ -196,11 +197,20 @@
     target = jnp.floor((assigned + 0.5) * (1.0 / SLOTS))
     slot = assigned - target * SLOTS + 1.0
     cost = cost_ref[...].astype(F32)
+    eye = one_hot(iota((COLS, COLS), 0) == iota((COLS, COLS), 1))
+    target_col = dot_nt(eye, jnp.broadcast_to(target, (8, COLS)).astype(BF16))[:, 0:1]
+    sooner = iota((COLS, COLS), 0) < iota((COLS, COLS), 1)
+    rank = jnp.sum(jnp.where(sooner & (target_col == target), 1.0, 0.0), axis=0, keepdims=True)
+    to_x = jnp.floor((target + 0.5) * (1.0 / (2 * nz)))
+    rest = target - to_x * (2 * nz)
+    to_z = jnp.floor((rest + 0.5) * 0.5)
+    kind = to_x * 2.0 + (rest - to_z * 2.0)
+    place = to_z * cap2 + (me * cap).astype(F32) + rank
     sub = iota((LANES, COLS), 0)
-    labels = jnp.where(sub == LANE_TARGET, target, 0.0)
+    labels = jnp.where(sub == LANE_PLACE, place, 0.0)
+    labels = jnp.where(sub == LANE_CLASS, kind, labels)
     labels = jnp.where(sub == LANE_SLOT, slot, labels)
     labels = jnp.where(sub == LANE_COST, cost, labels).astype(BF16)
-    eye = one_hot(iota((COLS, COLS), 0) == iota((COLS, COLS), 1))
     payload = temper + pltpu.roll(vapour, 64, 1) + dot_nt(eye, labels)
     got1[me] = payload.astype(BF16)
 
@@ -211,7 +221,7 @@
 
     @pl.when(core == 0)
     def _():
-        pl.semaphore_wait(barrier, 2 * nx - 1 + 2)
+        pl.semaphore_wait(barrier, 2 * nx - 1)
         announce(plane_in, sibling)
 
     @pl.when(core == 1)
@@ -228,7 +238,8 @@
             device_id_type=MESH,
         )
 
-    for o in range(1, n_near):
+    near_order = sorted(range(1, n_near), key=lambda o: -min(o, n_near - o))
+    for o in near_order:
         copy1(o).start()
 
     def edge_copies(turn):
@@ -287,11 +298,28 @@
         both = jnp.concatenate([half_in[:, tile(left)], half_in[:, tile(right)]], axis=1)
         out = dot(both, regroup[j % 2])
         state_a[0:80, tile(j + 1)] = out[:, 0:LANES]
-        drive[:, tile(j)] = out[:, LANES:]
+        drive[:, tile(j)] = 0.3 * out[:, LANES:]
     srow = iota((LANES, LANES), 0) & 63
     scol = iota((LANES, LANES), 1) & 1
     for j in range(HALF):
         spread[:, tile(j)] = one_hot(srow == j + HALF * scol)
+    odd_lane = (iota((8, LANES), 1) & 1) == 1
+
+    def ends(source, rows):
+        first, final = source[rows, tile(1)], source[rows, tile(HALF)]
+        source[rows, tile(0)] = jnp.where(odd_lane, pltpu.roll(final, 1, 1), first)
+        source[rows, tile(HALF + 1)] = jnp.where(odd_lane, final, pltpu.roll(first, LANES - 1, 1))
+
+    def mix(source, rows, j):
+        own = source[rows, tile(j + 1)]
+        beside = pltpu.roll(own, 2, 1) + pltpu.roll(own, LANES - 2, 1)
+        return 0.2 * (own + source[rows, tile(j)] + source[rows, tile(j + 2)] + beside)
+
+    for g in range(2 * SLOTS // 8):
+        rows = slice(8 * g, 8 * g + 8)
+        ends(state_a, rows)
+        for j in range(HALF):
+            state_b[rows, tile(j + 1)] = mix(state_a, rows, j) - drive[rows, tile(j)]
     first_means = dot_nt(state_a[0:80, LANES : LANES + WIDE].astype(BF16), spread[...])
 
     @pl.when(core == 1)
@@ -299,23 +327,17 @@
         pl.semaphore_wait(barrier, 2 * nz - 1 + 2)
         announce(line_in, sibling)
 
-    dynamics_send(0)
 
     for o in range(1, n_near):
         copy1(o).wait_recv()
     plane = got1[...].reshape(rows1, LANES)
     pick_row = iota((8, LANES), 0)
     pick_lane = iota((8, LANES), 1)
-    picker = one_hot(pick_lane == LANE_TARGET + pick_row)
-    owner = dot_nt(picker, plane)[0:1, :]
-    zid = iota((nz, rows1), 0)
-    mine = owner == (x * (2 * nz) + 2 * zid + core).astype(F32)
-    hits = jnp.where(mine, 1.0, 0.0)
-    before = one_hot(iota((rows1, rows1), 0) < iota((rows1, rows1), 1))
-    earlier = dot(hits.astype(BF16), before)
-    place = jnp.sum(hits * (zid.astype(F32) * cap2 + earlier + 1.0), axis=0, keepdims=True) - 1.0
-    packer = jnp.where(iota((rows2, rows1), 0).astype(F32) == place, 1.0, 0.0)
-    pack2[...] = dot(packer.astype(BF16), plane).astype(BF16).reshape(pack2.shape)
+    picker = one_hot(pick_lane == LANE_PLACE + pick_row)
+    labels = dot_nt(picker, plane)
+    place = jnp.where(labels[1:2, :] == me.astype(F32), labels[0:1, :], -1.0)
+    packer = one_hot(iota((rows2, rows1), 0).astype(F32) == place)
+    pack2[...] = dot(packer, plane).astype(BF16).reshape(pack2.shape)
 
     def copy_far(o, src, dst, send, recv):
         to = (z + o) % nz
@@ -336,7 +358,10 @@
     for o in order:
         copy_far(o, pack2, got2, s2, r2).start()
     got2[z] = pack2[z]
-    unpacker = packer.T.astype(BF16)
+    dynamics_send(0)
+    class_col = plane[:, LANE_CLASS : LANE_CLASS + 1].astype(F32)
+    place_col = jnp.where(class_col == me.astype(F32), plane[:, LANE_PLACE : LANE_PLACE + 1].astype(F32), -1.0)
+    unpacker = one_hot(iota((rows1, rows2), 1).astype(F32) == place_col)
 
     dynamics_finish(0)
     dynamics_send(1)
@@ -344,7 +369,7 @@
     for o in order:
         copy_far(o, pack2, got2, s2, r2).wait_recv()
     arrived = got2[...].reshape(rows2, LANES)
-    slot_row = dot_nt(picker, arrived)[1:2, :]
+    slot_row = dot_nt(picker, arrived)[2:3, :]
     matcher = one_hot((iota((SLOTS, rows2), 0) + 1).astype(F32) == slot_row)
     forcing = dot(matcher, arrived)
     slot_col = arrived[:, LANE_SLOT : LANE_SLOT + 1].astype(F32)
@@ -353,7 +378,7 @@
     stacked = jnp.concatenate(
         [jnp.where(slot_lane < 64, forcing, 0.0), jnp.where(slot_lane < 64, 0.0, forcing)], axis=0
     ).astype(BF16)
-    drive[...] = 0.3 * (dot(stacked, spread[...]) - drive[...])
+    forced[...] = 0.3 * dot(stacked, spread[...])
     near_counts = jnp.broadcast_to(forcing[:, LANE_COST : LANE_COST + 1], (SLOTS, LANES))
     tend[...] = jnp.zeros_like(tend)
     tend[0:SLOTS, 0:LANES] = near_counts
@@ -361,32 +386,25 @@
     def slot_group(g):
         top, low, last = (slice(8 * g + 40 * k, 8 * g + 40 * k + 8) for k in range(3))
         steps = tend[top, 0:LANES]
-        is_odd = (iota((8, LANES), 1) & 1) == 1
-        slope = jnp.where(is_odd, 0.4, 0.0)
+        slope = jnp.where(odd_lane, 0.4, 0.0)
         source, sink = state_a, state_b
         for n in range(NSUB):
             active = steps > n + 0.5
-            for rows in (top, low):
-                first, final = source[rows, tile(1)], source[rows, tile(HALF)]
-                source[rows, tile(0)] = jnp.where(is_odd, pltpu.roll(final, 1, 1), first)
-                source[rows, tile(HALF + 1)] = jnp.where(is_odd, final, pltpu.roll(first, LANES - 1, 1))
+            if n > 0:
+                for rows in (top, low):
+                    ends(source, rows)
             for j in range(HALF):
-                now, mixed = [], []
+                mixed = []
                 for rows in (top, low):
-                    own = source[rows, tile(j + 1)]
-                    around = (
-                        own
-                        + source[rows, tile(j)]
-                        + source[rows, tile(j + 2)]
-                        + pltpu.roll(own, 2, 1)
-                        + pltpu.roll(own, LANES - 2, 1)
-                    )
-                    now.append(own)
-                    mixed.append(0.2 * around + drive[rows, tile(j)])
+                    if n == 0:
+                        mixed.append(state_b[rows, tile(j + 1)] + forced[rows, tile(j)])
+                        drive[rows, tile(j)] = forced[rows, tile(j)] - drive[rows, tile(j)]
+                    else:
+                        mixed.append(mix(source, rows, j) + drive[rows, tile(j)])
                 sat = ((0.5 - 0.8 * j / CZ) - slope) + 0.2 * mixed[0]
                 moved = 0.5 * jnp.maximum(mixed[1] - sat, 0.0)
-                t_new = jnp.where(active, mixed[0] + moved, now[0])
-                w_new = jnp.where(active, mixed[1] - moved, now[1])
+                t_new = jnp.where(active, mixed[0] + moved, source[top, tile(j + 1)])
+                w_new = jnp.where(active, mixed[1] - moved, source[low, tile(j + 1)])
                 sink[top, tile(j + 1)] = t_new
                 sink[low, tile(j + 1)] = w_new
                 if n == NSUB - 1:
@@ -445,7 +463,7 @@
             device_id_type=MESH,
         )
 
-    for o in range(1, n_near):
+    for o in near_order:
         copy4(o).start()
     got4[me] = pack4[me]
 
@@ -537,6 +555,7 @@
             pltpu.VMEM((n_near, COLS, 2 * LANES), BF16),
             pltpu.VMEM((120, WIDE + 2 * LANES), F32),
             pltpu.VMEM((120, WIDE + 2 * LANES), F32),
+            pltpu.VMEM((80, WIDE), F32),
             pltpu.VMEM((80, WIDE), F32),
             pltpu.VMEM((80, WIDE), BF16),
             pltpu.VMEM((LANES, WIDE), BF16),

time: 54 us -> 50.1 us (0.928)
  Pallas kernels: 53.2 us -> 49.3 us
    pallas_call x1, Pallas kernels: 51.4 us -> 47.5 us  [body(): pl.pallas_call(functools.partial(kernel, dims), out_shape=(jax.ShapeDtype...]
where the time goes in v4:
time: 50.1 us; the launch traced here: 50 us
  Pallas kernels  49.3 us (98%)
  between operations  0.64 us (1%)
    pallas_call x1, Pallas kernels, body(): pl.pallas_call(functools.partial(kernel, dims), out_shape=(jax.ShapeDtype...  47.5 us
    pallas_call x1, Pallas kernels, body(): pl.pallas_call(hand_over, out_shape=(jax.ShapeDtypeStruct(gcm.shape, F32)...  1.83 us

profile of v4, /device:TPU:1, one launch (start us, length us, event | category | flops | bytes accessed | tf_op | source)
XLA Modules:
  0.0 50.0 jit_solution(10406855874651808922)
XLA Ops:
  0.6 47.5 %physics_and_dynamics.1 = (f32[3,2,1152]{2,1,0:T(2,128)}, bf16[40,2,3712]{2,1,0:T(2,128)(2,1)}) custom-call(f32[3,2,1152]{2,1,0:T(2,128)} %bitcast.4, f32[2,16,16]{2,1,0:T(8,128)} %op_hbm.1, s32[2,4]{1,0:T(2,128)} %nb_hbm.1, bf16[40,2,3712]{2,1,0:T(2,128)(2,1)} %crm_hbm.1, s32[1,32]{1,0:T(1,128)} %bitcast.5, s32[1,32]{1,0:T(1,128)} %bitcast.6), custom_call_target="tpu_custom_call" | custom-call | tf_op jit(solution)/shard_map/physics_and_dynamics/pallas_call | solution.py:527
  48.1 1.8 %hand_over.1 = (f32[3,2,1152]{2,1,0:T(2,128)}, bf16[40,2,3712]{2,1,0:T(2,128)(2,1)}) custom-call(f32[3,2,1152]{2,1,0:T(2,128)} %get-tuple-element.6.gout_ref, bf16[40,2,3712]{2,1,0:T(2,128)(2,1)} %get-tuple-element.7.cout_ref), custom_call_target="tpu_custom_call" | custom-call | tf_op jit(solution)/shard_map/hand_over/pallas_call | solution.py:583

commit v5 on v4

--- a/solution.py
+++ b/solution.py
@@ -450,7 +450,11 @@
 
     for o in order:
         copy_far(o, pack3, got3, s3, r3).wait_recv()
-    pack4[...] = dot(unpacker, got3[...].reshape(rows2, 256)).astype(BF16).reshape(pack4.shape)
+    home = dot(unpacker, got3[...].reshape(rows2, 2 * LANES)).reshape(n_near, COLS, 2 * LANES)
+    pack4[:, 0:COLS] = home[:, :, 0:LANES].astype(BF16)
+    water = home[:, :, LANES:]
+    first_half = iota((n_near, 16, LANES), 2) < 64
+    pack4[:, COLS:48] = jnp.where(first_half, water[:, 0:16], water[:, 16:32]).astype(BF16)
 
     def copy4(o):
         to = (me + o) % n_near
@@ -474,9 +478,10 @@
     col = got4[0].astype(F32)
     for k in range(1, n_near):
         col = col + got4[k].astype(F32)
-    temper = jnp.where(lane < CZ, col[:, 0:LANES], 0.0)
-    vapour = jnp.where(lane < CZ, pltpu.roll(col[:, 0:LANES], 64, 1), 0.0)
-    cloud = jnp.where(lane < CZ, col[:, LANES:], 0.0)
+    temper = jnp.where(lane < CZ, col[0:COLS], 0.0)
+    vapour = jnp.where(lane < CZ, pltpu.roll(col[0:COLS], 64, 1), 0.0)
+    water = jnp.concatenate([col[COLS:48], pltpu.roll(col[COLS:48], 64, 1)], axis=0)
+    cloud = jnp.where(lane < CZ, water, 0.0)
     gained = jnp.concatenate([temper, vapour, cloud], axis=1) + base[...]
     result = dyn[...] + gained.astype(BF16).astype(F32).reshape(dyn.shape)
     for f in range(3):
@@ -551,8 +556,8 @@
             pltpu.VMEM((nz, cap2, LANES), BF16),
             pltpu.VMEM((nz, cap2, 2 * LANES), BF16),
             pltpu.VMEM((nz, cap2, 2 * LANES), BF16),
-            pltpu.VMEM((n_near, COLS, 2 * LANES), BF16),
-            pltpu.VMEM((n_near, COLS, 2 * LANES), BF16),
+            pltpu.VMEM((n_near, 48, LANES), BF16),
+            pltpu.VMEM((n_near, 48, LANES), BF16),
             pltpu.VMEM((120, WIDE + 2 * LANES), F32),
             pltpu.VMEM((120, WIDE + 2 * LANES), F32),
             pltpu.VMEM((80, WIDE), F32),

time: 50.1 us -> 50 us (level)
  no operation moved by 1% of the time
where the time goes in v5:
time: 50 us; the launch traced here: 49.9 us
  Pallas kernels  49.2 us (98%)
  between operations  0.64 us (1%)
    pallas_call x1, Pallas kernels, body(): pl.pallas_call(functools.partial(kernel, dims), out_shape=(jax.ShapeDtype...  47.4 us
    pallas_call x1, Pallas kernels, body(): pl.pallas_call(hand_over, out_shape=(jax.ShapeDtypeStruct(gcm.shape, F32)...  1.83 us

profile of v5, /device:TPU:1, one launch (start us, length us, event | category | flops | bytes accessed | tf_op | source)
XLA Modules:
  0.0 49.9 jit_solution(15722013445224263055)
XLA Ops:
  0.6 47.4 %physics_and_dynamics.1 = (f32[3,2,1152]{2,1,0:T(2,128)}, bf16[40,2,3712]{2,1,0:T(2,128)(2,1)}) custom-call(f32[3,2,1152]{2,1,0:T(2,128)} %bitcast.4, f32[2,16,16]{2,1,0:T(8,128)} %op_hbm.1, s32[2,4]{1,0:T(2,128)} %nb_hbm.1, bf16[40,2,3712]{2,1,0:T(2,128)(2,1)} %crm_hbm.1, s32[1,32]{1,0:T(1,128)} %bitcast.5, s32[1,32]{1,0:T(1,128)} %bitcast.6), custom_call_target="tpu_custom_call" | custom-call | tf_op jit(solution)/shard_map/physics_and_dynamics/pallas_call | solution.py:532
  48.0 1.8 %hand_over.1 = (f32[3,2,1152]{2,1,0:T(2,128)}, bf16[40,2,3712]{2,1,0:T(2,128)(2,1)}) custom-call(f32[3,2,1152]{2,1,0:T(2,128)} %get-tuple-element.6.gout_ref, bf16[40,2,3712]{2,1,0:T(2,128)(2,1)} %get-tuple-element.7.cout_ref), custom_call_target="tpu_custom_call" | custom-call | tf_op jit(solution)/shard_map/hand_over/pallas_call | solution.py:588
